TPU v7x, 256 devices: a whole 4x4x8 slice. The times are simulated.
256 devices in a mesh: passage: 32 (over x, z_hi, core), span: 8 (over z_lo, y).
Axes of the slice: x: 4, y: 4, z: 8 (z_hi: 4, z_lo: 2; z = z_hi * 2 + z_lo), core: 2. Of those that a mesh axis runs over, the one named last changes fastest.
Arguments:
- state: float32 [7, 32, 48, 128, 128], P(None, 'passage', None, 'span'), may hold values from -6 to 6
- previous: float32 [7, 32, 48, 128, 128], P(None, 'passage', None, 'span'), may hold values from -6 to 6
- earlier: float32 [7, 32, 48, 128, 128], P(None, 'passage', None, 'span'), may hold values from -6 to 6
- axial_speed: float32 [32, 48, 128, 128], P('passage', None, 'span'), may hold values from 0.2 to 1
- pitch_speed: float32 [32, 48, 128, 128], P('passage', None, 'span'), may hold values from -0.6 to 0.6
- viscosity: float32 [32, 48, 128, 128], P('passage', None, 'span'), may hold values from 0.02 to 0.2
- inflow: float32 [7, 128, 128], P(None, 'span'), may hold values from -6 to 6
- coupling: float32 [7, 7], replicated, may hold values from -2 to 2
- partner: int32 [32], replicated, may hold values from 0 to 31, as said below
- tile_ids: int32 [32, 8, 4], replicated, may hold values from 0 to 255, as said below
- tile_weights: int32 [32, 8, 4], replicated, may hold values from 1 to 16
Outputs:
- updated: float32 [7, 32, 48, 128, 128], P(None, 'passage', None, 'span')
Inputs may be any that keep to these rules, and one draw needn't show every extreme that they name: `partner`: rotor passages' partners form one cycle through all rotor passages, stator passages' partners one cycle through all stator passages; each cycle gives its row's order around the annulus. `tile_ids`: A rotor passage's tiles list tiles of stator passages and a stator passage's tiles list tiles of rotor passages; each list names 4 consecutive tiles of the other row, taken in that row's annulus order (its partner cycle, tiles of a passage in order), cyclically; every tile is named by exactly 4 lists, and tile a lists tile b exactly when b lists a.
All inputs are finite; a program needn't handle non-finite values.
Results may differ from a plain program's by a relative error of at most 0.00005.
Values sent between devices are 32-bit elements; how exact they have to be, the bound alone decides.
No kernel may reach another device: no remote copies, remote signals or barrier semaphores. Data moves between devices by JAX's collectives and lax.ppermute only.
A program may use at most 128 MiB of HBM per device.

v0:
```python
import jax
import jax.numpy as jnp
from jax import lax
from jax.sharding import PartitionSpec as P

CFL = 0.8
STEP_DT = 2.0
FIRST = 0.5
SECOND = 1.0
HIGHEST = lax.Precision.HIGHEST


def padded(cells, sides, width):
    for axis, dim in sides:
        count = lax.axis_size(axis)
        ends = count - 1
        head = lax.slice_in_dim(cells, 0, width, axis=dim)
        tail = lax.slice_in_dim(cells, cells.shape[dim] - width, cells.shape[dim], axis=dim)
        cells = jnp.concatenate(
            [
                lax.ppermute(tail, axis, [(i, (i + 1) % count) for i in range(ends)]),
                cells,
                lax.ppermute(head, axis, [((i + 1) % count, i) for i in range(ends)]),
            ],
            axis=dim,
        )
    return cells


def residual(
    current,
    inlet_ghost,
    outlet_ghost,
    below_ghost,
    above_ghost,
    spanned,
    prior,
    older,
    speed_axial,
    speed_pitch,
    diffusion,
    coupling,
):
    axial_line = jnp.concatenate([inlet_ghost[:, None], current, outlet_ghost[:, None]], axis=1)
    pitch_line = jnp.concatenate([below_ghost[..., None], current, above_ghost[..., None]], axis=3)
    forward_axial = axial_line[:, 2:]
    backward_axial = axial_line[:, :-2]
    forward_pitch = pitch_line[..., 2:]
    backward_pitch = pitch_line[..., :-2]
    doubled = 2.0 * current
    spread = (
        forward_axial
        - doubled
        + backward_axial
        + (forward_pitch - doubled + backward_pitch)
        + (spanned[:, :, 2:] - doubled + spanned[:, :, :-2])
    )
    transport = 0.5 * speed_axial * (forward_axial - backward_axial) + 0.5 * speed_pitch * (
        forward_pitch - backward_pitch
    )
    mixing = jnp.einsum("fg,gasp->fasp", coupling, current, precision=HIGHEST)
    unsteady = (3.0 * current - 4.0 * prior + older) / (2.0 * STEP_DT)
    return unsteady + transport - diffusion * spread + mixing


def on_device(
    state,
    previous,
    earlier,
    axial_speed,
    pitch_speed,
    viscosity,
    inflow,
    coupling,
    partner,
    tile_ids,
    tile_weights,
):
    own_index = lax.axis_index("passage")
    row_count = lax.axis_size("passage") // 2
    rotor_side = (own_index + (own_index >= row_count).astype(jnp.int32)) % 4 < 2
    fields, _, axial_cells, span_cells, pitch_cells = state.shape
    tiles_per = tile_ids.shape[1]
    own_ids = lax.dynamic_index_in_dim(tile_ids, own_index, 0, keepdims=False)
    own_weights = lax.dynamic_index_in_dim(tile_weights, own_index, 0, keepdims=False).astype(
        jnp.float32
    )
    shares = own_weights / jnp.sum(own_weights, axis=1, keepdims=True)
    upper_partner = lax.dynamic_index_in_dim(partner, own_index, 0, keepdims=False)
    prior = previous[:, 0]
    older = earlier[:, 0]
    speed_axial = axial_speed[0]
    speed_pitch = pitch_speed[0]
    diffusion = viscosity[0]
    pseudo_dt = CFL / (speed_axial + jnp.abs(speed_pitch) + 6.0 * diffusion + 1.5 / STEP_DT)

    def gather_edges(edge_piece):
        piece_count = edge_piece.shape[0]
        indices = jnp.arange(piece_count, dtype=jnp.int32)
        takes_above = (indices == upper_partner)[:, None, None]
        takes_below = (partner == own_index)[:, None, None]
        below_sum = jnp.sum(jnp.where(takes_below, edge_piece[:, 1], 0.0), axis=0)
        above_sum = jnp.sum(jnp.where(takes_above, edge_piece[:, 0], 0.0), axis=0)
        return (below_sum, above_sum)

    def gather_tiles(face_piece):
        piece_count = face_piece.shape[0]
        columns = jnp.arange(piece_count * tiles_per, dtype=jnp.int32)
        selected = (own_ids[:, :, None] == columns).astype(jnp.float32)
        weight_block = jnp.sum(shares[:, :, None] * selected, axis=1).reshape(
            tiles_per, piece_count, tiles_per
        )
        blocks = face_piece.reshape(
            piece_count, fields, span_cells, tiles_per, pitch_cells // tiles_per
        )
        return jnp.einsum("tmu,mfsuv->fstv", weight_block, blocks, precision=HIGHEST)

    def advance(current, factor):
        cells = current[:, 0]
        spanned = padded(current, (("span", 3),), 1)[:, 0]
        edges = jnp.stack([cells[:, :, :, 0], cells[:, :, :, -1]], axis=0).reshape(
            1, 2, fields, axial_cells * span_cells
        )
        exit_face = jnp.where(rotor_side, cells[:, -1], cells[:, 0])[None]
        below_flat, above_flat = gather_edges(lax.all_gather(edges, "passage", axis=0, tiled=True))
        sliding = gather_tiles(lax.all_gather(exit_face, "passage", axis=0, tiled=True))
        sliding = sliding.reshape(fields, span_cells, pitch_cells)
        inlet_ghost = jnp.where(rotor_side, inflow, sliding)
        outlet_ghost = jnp.where(rotor_side, sliding, cells[:, -1])
        below_ghost = below_flat.reshape(fields, axial_cells, span_cells)
        above_ghost = above_flat.reshape(fields, axial_cells, span_cells)
        change = residual(
            cells,
            inlet_ghost,
            outlet_ghost,
            below_ghost,
            above_ghost,
            spanned,
            prior,
            older,
            speed_axial,
            speed_pitch,
            diffusion,
            coupling,
        )
        return (cells - factor * pseudo_dt * change)[:, None]

    middle = advance(state, FIRST)
    return advance(middle, SECOND)


def solution(mesh):
    placed = (
        P(None, "passage", None, "span", None),
        P(None, "passage", None, "span", None),
        P(None, "passage", None, "span", None),
        P("passage", None, "span", None),
        P("passage", None, "span", None),
        P("passage", None, "span", None),
        P(None, "span", None),
        P(),
        P(),
        P(),
        P(),
    )
    return jax.shard_map(
        on_device,
        mesh=mesh,
        in_specs=placed,
        out_specs=P(None, "passage", None, "span", None),
        check_vma=False,
    )
```

profile of v0, /device:TPU:1, one launch (start us, length us, event | category | flops | bytes accessed | tf_op | source)
XLA Modules:
  0.0 359.5 jit_solution(4358453427725039442)
XLA Ops:
  6.5 3.4 copy.244
  9.9 3.9 %fusion.45 = (f32[7,48,16,1]{3,0,2,1:T(8,128)}, f32[7,48,16,1]{3,0,2,1:T(8,128)}) fusion(f32[7,48,16,128]{3,0,2,1:T(8,128)S(1)} %bitcast.125), kind=kLoop, calls=%fused_computation.86 | loop fusion | bytes 86016 | tf_op jit(solution)/shard_map/slice | solution.py:121
  13.8 3.5 copy.148
  17.5 3.5 copy.149
  21.2 0.6 copy.150
  22.7 0.8 fusion.46
  23.4 4.0 %collective-permute-start = (f32[7,1,48,1,128]{4,0,3,2,1:T(8,128)}, f32[7,1,48,1,128]{4,0,3,2,1:T(8,128)S(1)}, u32[]{:S(2)}, u32[]{:S(2)}) collective-permute-start(f32[7,1,48,1,128]{4,0,3,2,1:T(8,128)} %get-tuple-element.13), channel_id=1, source_target_pairs={{0,1},{1,2},{2,3},{3,4},{4,5},{5,6},{6,7},{8,9},{9,10},{10,11},{11... | collective-permute-start | bytes 516104 | tf_op jit(solution)/shard_map/ppermute | solution.py:21
  27.5 1.3 collective-permute-start.1
  29.5 0.7 copy.172
  31.4 2.5 fusion.41
  33.9 1.3 collective-permute-done.1
  35.1 3.0 maximum_bitcast_fusion
  38.1 40.8 %all-gather.7.cloned.1.call-done = f32[32,2,7,768]{3,1,2,0:T(2,128)} async-done(((f32[1,2,7,768]{3,1,2,0:T(2,128)}), f32[32,2,7,768]{3,1,2,0:T(2,128)}) %all-gather.7.cloned.1.call-update) | async-done | bytes 1376272 | tf_op jit(solution)/shard_map/all_gather | solution.py:125
  79.0 3.0 fusion.49
  82.3 3.5 copy.152
  85.9 3.3 copy.154
  89.2 43.5 %all-gather.11.cloned.1.call-done = f32[224,1,16,128]{3,2,1,0:T(8,128)} async-done(((f32[7,1,16,128]{3,2,1,0:T(8,128)}), f32[224,1,16,128]{3,2,1,0:T(8,128)}) %all-gather.11.cloned.1.call-update) | async-done | bytes 1835024 | tf_op jit(solution)/shard_map/all_gather | solution.py:126
  132.7 9.3 %reshape.101 = f32[32,7,16,8,16]{4,3,2,1,0:T(8,128)} reshape(f32[224,1,16,128]{3,2,1,0:T(8,128)} %all-gather.11.cloned.1.call-done) | data formatting | bytes 3670016 | tf_op jit(solution)/shard_map/reshape | solution.py:113
  142.0 21.1 %fusion.23 = f32[7,16,8,16]{3,2,1,0:T(8,128)} fusion(f32[8,32,8,1,1]{1,0,2,4,3:T(8,128)} %copy.172, f32[32,7,16,8,16]{4,3,2,1,0:T(8,128)} %reshape.101), kind=kOutput, calls=%fused_computation.44 | convolution fusion | flops 44040192 | bytes 1900544 | tf_op jit(solution)/shard_map/tmu,mfsuv->fstv/dot_general | solution.py:116
  163.1 1.8 reshape.103
  164.9 1.8 reshape.104
  166.7 1.5 copy_select_fusion.3
  168.2 1.5 fusion.37
  169.7 13.6 %fusion.16 = f32[7,48,16,128]{3,0,2,1:T(8,128)S(1)} fusion(f32[7,48,16,128]{3,0,2,1:T(8,128)S(1)} %bitcast.128, f32[7,48,18,128]{3,0,2,1:T(8,128)} %maximum_bitcast_fusion, f32[7,1,48,16,128]{4,3,2,1,0:T(8,128)} %param.13, f32[7,48,16,1]{3,0,2,1:T(8,128)} %copy.152, f32[7,48,16,1]{3,0,2,1:T(8,128)} %copy.154, f32[7,1,16,128]{3,0,2,1:T(8,128)} %copy_select_fusion.3, ...), kind=kOutput, calls=%fused_computation.25 | convolution fusion | flops 77758464 | bytes 21788672 | tf_op jit(solution)/shard_map/fg,gasp->fasp/dot_general | solution.py:61
  183.3 3.9 %fusion.43 = (f32[7,48,16,1]{3,0,2,1:T(8,128)}, f32[7,48,16,1]{3,0,2,1:T(8,128)}) fusion(f32[7,48,16,128]{3,0,2,1:T(8,128)S(1)} %fusion.16), kind=kLoop, calls=%fused_computation.84 | loop fusion | bytes 86016 | tf_op jit(solution)/shard_map/slice | solution.py:121
  187.2 3.7 %copy.164 = f32[7,48,16,1]{2,1,3,0:T(8,128)S(1)} copy(f32[7,48,16,1]{3,0,2,1:T(8,128)} %get-tuple-element.7) | data formatting | bytes 43008 | tf_op jit(solution)/shard_map/slice | solution.py:121
  191.0 3.5 copy.165
  194.7 0.6 copy.166
  195.5 0.6 copy.158
  196.1 3.1 collective-permute-start.2
  199.3 1.3 collective-permute-start.3
  200.6 2.7 collective-permute-done.2
  203.3 3.8 %collective-permute-done.3 = f32[7,1,48,1,128]{4,0,3,2,1:T(8,128)S(1)} collective-permute-done((f32[7,1,48,1,128]{4,0,3,2,1:T(8,128)S(1)}, f32[7,1,48,1,128]{4,0,3,2,1:T(8,128)S(1)}, u32[]{:S(2)}, u32[]{:S(2)}) %collective-permute-start.3) | collective-permute-done | bytes 172064 | tf_op jit(solution)/shard_map/ppermute | solution.py:23
  207.1 2.1 maximum_bitcast_fusion.1
  209.2 36.4 %all-gather.9.cloned.1.call-done = f32[32,2,7,768]{3,1,2,0:T(2,128)} async-done(((f32[1,2,7,768]{3,1,2,0:T(2,128)}), f32[32,2,7,768]{3,1,2,0:T(2,128)}) %all-gather.9.cloned.1.call-update) | async-done | bytes 1376272 | tf_op jit(solution)/shard_map/all_gather | solution.py:125
  245.6 3.8 %fusion.48 = (f32[32,1,7,768]{3,1,2,0:T(1,128)S(1)}, f32[32,1,7,768]{3,1,2,0:T(1,128)}) fusion(f32[32,2,7,768]{3,1,2,0:T(2,128)} %all-gather.9.cloned.1.call-done), kind=kLoop, calls=%fused_computation.89 | loop fusion | bytes 2752512 | tf_op jit(solution)/shard_map/slice | solution.py:102
  249.7 3.5 copy.170
  253.2 1.3 fusion.32
  254.6 3.3 copy.168
  257.9 41.3 %all-gather.13.cloned.1.call-done = f32[224,1,16,128]{3,2,1,0:T(8,128)} async-done(((f32[7,1,16,128]{3,2,1,0:T(8,128)}), f32[224,1,16,128]{3,2,1,0:T(8,128)}) %all-gather.13.cloned.1.call-update) | async-done | bytes 1835024 | tf_op jit(solution)/shard_map/all_gather | solution.py:126
  299.2 9.3 %reshape.105 = f32[32,7,16,8,16]{4,3,2,1,0:T(8,128)} reshape(f32[224,1,16,128]{3,2,1,0:T(8,128)} %all-gather.13.cloned.1.call-done) | data formatting | bytes 3670016 | tf_op jit(solution)/shard_map/reshape | solution.py:113
  308.5 21.1 %fusion.26 = f32[7,16,8,16]{3,2,1,0:T(8,128)} fusion(f32[8,32,8,1,1]{1,0,2,4,3:T(8,128)} %copy.172, f32[32,7,16,8,16]{4,3,2,1,0:T(8,128)} %reshape.105), kind=kOutput, calls=%fused_computation.45 | convolution fusion | flops 44040192 | bytes 1900544 | tf_op jit(solution)/shard_map/tmu,mfsuv->fstv/dot_general | solution.py:116
  329.6 1.8 reshape.106
  331.4 1.8 reshape.107
  333.2 1.5 copy_select_fusion.2
  334.7 1.5 fusion.38
  336.2 14.2 %fusion.10 = f32[7,1,48,16,128]{4,0,3,2,1:T(8,128)S(1)} fusion(f32[7,48,16,128]{3,0,2,1:T(8,128)S(1)} %copy-done.3, f32[7,48,18,128]{3,0,2,1:T(8,128)} %maximum_bitcast_fusion.1, f32[7,1,48,16,128]{4,3,2,1,0:T(8,128)} %param.13, f32[7,48,16,1]{3,0,2,1:T(8,128)} %copy.168, f32[7,48,16,1]{3,0,2,1:T(8,128)} %copy.170, ...), kind=kOutput, calls=%fused_computation.13 | convolution fusion | flops 77758464 | bytes 21784772 | tf_op jit(solution)/shard_map/fg,gasp->fasp/dot_general | solution.py:61
  350.4 2.0 copy.171
  (53 shorter events, 4.2 us)
Async XLA Ops:
  6.5 22.6 %copy-start = (s32[32,8,4]{0,2,1:T(4,128)S(1)}, s32[32,8,4]{0,2,1:T(4,128)}, u32[]{:S(2)}) copy-start(s32[32,8,4]{0,2,1:T(4,128)} %param.20) | copy-start | bytes 12292
  6.5 72.4 %all-gather.7.cloned.1.call-start = ((), (), s32[]{:S(2)}) async-start(), calls=%async_computation | async-start | bytes 1419264 | tf_op jit(solution)/shard_map/all_gather | solution.py:125
  17.4 11.4 %copy-start.6 = (s32[32,8,4]{0,2,1:T(4,128)S(1)}, s32[32,8,4]{0,2,1:T(4,128)}, u32[]{:S(2)}) copy-start(s32[32,8,4]{0,2,1:T(4,128)} %param.21) | copy-start | bytes 12292
  17.4 12.9 %copy-start.8 = (s32[32]{0:T(128)S(1)}, s32[32]{0:T(128)}, u32[]{:S(2)}) copy-start(s32[32]{0:T(128)} %param.19) | copy-start | bytes 388
  21.9 110.8 %all-gather.11.cloned.1.call-start = ((), (), s32[]{:S(2)}) async-start(), calls=%async_computation.2 | async-start | bytes 1892352 | tf_op jit(solution)/shard_map/all_gather | solution.py:126
  22.6 223.0 %all-gather.9.cloned.1.call-start = ((), (), s32[]{:S(2)}) async-start(), calls=%async_computation.1 | async-start | bytes 1419264 | tf_op jit(solution)/shard_map/all_gather | solution.py:125
  23.4 10.4 %collective-permute-start = (f32[7,1,48,1,128]{4,0,3,2,1:T(8,128)}, f32[7,1,48,1,128]{4,0,3,2,1:T(8,128)S(1)}, u32[]{:S(2)}, u32[]{:S(2)}) collective-permute-start(f32[7,1,48,1,128]{4,0,3,2,1:T(8,128)} %get-tuple-element.13), channel_id=1, source_target_pairs={{0,1},{1,2},{2,3},{3,4},{4,5},{5,6},{6,7},{8,9},{9,10},{10,11},{11... | collective-permute-start | bytes 516104 | tf_op jit(solution)/shard_map/ppermute | solution.py:21
  27.5 7.7 %collective-permute-start.1 = (f32[7,1,48,1,128]{4,0,3,2,1:T(8,128)}, f32[7,1,48,1,128]{4,0,3,2,1:T(8,128)}, u32[]{:S(2)}, u32[]{:S(2)}) collective-permute-start(f32[7,1,48,1,128]{4,0,3,2,1:T(8,128)} %get-tuple-element.14), channel_id=1, source_target_pairs={{1,0},{2,1},{3,2},{4,3},{5,4},{6,5},{7,6},{9,8},{10,9},{11,10},{12... | collective-permute-start | bytes 516104 | tf_op jit(solution)/shard_map/ppermute | solution.py:23
  142.0 27.7 %copy-start.4 = (f32[1,48,16,128]{3,2,1,0:T(8,128)S(1)}, f32[1,48,16,128]{3,2,1,0:T(8,128)}, u32[]{:S(2)}) copy-start(f32[1,48,16,128]{3,2,1,0:T(8,128)} %param.16) | copy-start | bytes 1179652
  142.0 27.7 %copy-start.7 = (f32[7,7]{1,0:T(8,128)S(1)}, f32[7,7]{1,0:T(8,128)}, u32[]{:S(2)}) copy-start(f32[7,7]{1,0:T(8,128)} %param.18) | copy-start | bytes 592
  183.3 3.9 %copy-start.2 = (f32[7,48,16,128]{3,0,2,1:T(8,128)}, f32[7,48,16,128]{3,0,2,1:T(8,128)S(1)}, u32[]{:S(2)}) copy-start(f32[7,48,16,128]{3,0,2,1:T(8,128)S(1)} %fusion.16) | copy-start | bytes 8257540
  187.2 8.2 %copy-start.3 = (f32[7,48,16,128]{3,0,2,1:T(8,128)S(1)}, f32[7,48,16,128]{3,0,2,1:T(8,128)}, u32[]{:S(2)}) copy-start(f32[7,48,16,128]{3,0,2,1:T(8,128)} %copy-done.2) | copy-start | bytes 8257540
  195.4 103.8 %all-gather.13.cloned.1.call-start = ((), (), s32[]{:S(2)}) async-start(), calls=%async_computation.3 | async-start | bytes 1892352 | tf_op jit(solution)/shard_map/all_gather | solution.py:126
  196.1 7.1 %collective-permute-start.2 = (f32[7,1,48,1,128]{4,0,3,2,1:T(8,128)S(1)}, f32[7,1,48,1,128]{4,0,3,2,1:T(8,128)S(1)}, u32[]{:S(2)}, u32[]{:S(2)}) collective-permute-start(f32[7,1,48,1,128]{4,0,3,2,1:T(8,128)S(1)} %get-tuple-element.9), channel_id=1, source_target_pairs={{0,1},{1,2},{2,3},{3,4},{4,5},{5,6},{6,7},{8,9},{9,10},{10,11},{11... | collective-permute-start | bytes 516104 | tf_op jit(solution)/shard_map/ppermute | solution.py:21
  199.3 7.8 %collective-permute-start.3 = (f32[7,1,48,1,128]{4,0,3,2,1:T(8,128)S(1)}, f32[7,1,48,1,128]{4,0,3,2,1:T(8,128)S(1)}, u32[]{:S(2)}, u32[]{:S(2)}) collective-permute-start(f32[7,1,48,1,128]{4,0,3,2,1:T(8,128)S(1)} %get-tuple-element.10), channel_id=1, source_target_pairs={{1,0},{2,1},{3,2},{4,3},{5,4},{6,5},{7,6},{9,8},{10,9},{11,10},{12... | collective-permute-start | bytes 516104 | tf_op jit(solution)/shard_map/ppermute | solution.py:23
  308.5 27.7 %copy-start.5 = (f32[1,48,16,128]{3,2,1,0:T(8,128)S(1)}, f32[1,48,16,128]{3,2,1,0:T(8,128)}, u32[]{:S(2)}) copy-start(f32[1,48,16,128]{3,2,1,0:T(8,128)} %param.16) | copy-start | bytes 1179652
  336.2 16.3 %copy-start.1 = (s32[32,8,4]{0,2,1:T(4,128)S(1)}, s32[32,8,4]{0,2,1:T(4,128)}, u32[]{:S(2)}) copy-start(s32[32,8,4]{0,2,1:T(4,128)} %param.20) | copy-start | bytes 12292
Sparse Core Ops, SparseCore 0:
  22.0 56.9 all-gather.6
  81.5 51.1 all-gather.10
  195.5 50.0 all-gather.8
  248.0 51.1 all-gather.12
where the time goes:
time: 366 us; the launch traced here: 359 us
  waiting for transfers between devices  170 us (46%)
  local copies, waits for them, and re-layouts  79.6 us (22%)
  matrix products  70 us (19%)
  other arithmetic  16.2 us (4%)
  between operations  13.9 us (4%)
  starting transfers between devices  9.85 us (3%)
    all_gather x2, waiting for transfers between devices, advance(): lax.all_gather(exit_face, 'passage', axis=0, tiled=True)  84.8 us
    all_gather x2, waiting for transfers between devices, advance(): lax.all_gather(edges, 'passage', axis=0, tiled=True)  77.2 us
    dot_general x2, matrix products, gather_tiles(): jnp.einsum('tmu,mfsuv->fstv', weight_block, blocks, precision=HIGHEST)  42.2 us
    dot_general x2, matrix products, residual(): mixing = jnp.einsum('fg,gasp->fasp', coupling, current, precision=HIGHEST)  27.8 us
    reshape x2, local copies, waits for them, and re-layouts, gather_tiles(): face_piece.reshape(piece_count, fields, span_cells, tiles_per, pitch_cell...  18.6 us
    slice x4, local copies, waits for them, and re-layouts, advance(): cells[:, :, :, 0]  15 us
  transfers between devices with their start and end apart: 8, of which 7 were waited for; matrix products, arithmetic and copies ran while one was open for 10% of the time, Pallas kernels for 0%

commit v1 on v0

v1 whole, which is shorter than its diff:
```python
import functools

import jax
import jax.numpy as jnp
from jax import lax
from jax.experimental import pallas as pl
from jax.experimental.pallas import tpu as pltpu
from jax.sharding import PartitionSpec as P

CFL = 0.8
STEP_DT = 2.0

X_FLIPS = (8, 16, 24)
Z_FLIPS = (2, 4, 6)
CORE_FLIP = 1
SOURCES = (0, 8, 16, 24, 1, 9, 17, 25)
DESTS = (0, 2, 4, 6)

LAYERS = 8

SMEM = pl.BlockSpec(memory_space=pltpu.SMEM)
VMEM = pl.BlockSpec(memory_space=pltpu.VMEM)


def params():
    return pltpu.CompilerParams(vmem_limit_bytes=48 * 1024 * 1024)


def lanes(shape):
    return lax.broadcasted_iota(jnp.int32, shape, len(shape) - 1)


def pack_kernel(info, s_ref, packet_ref, low_ref, high_ref):
    fields, rows, width = s_ref.shape
    depth = rows // 16
    pair = lanes((8, width)) >> 1
    start = info[1] * (rows - 16)

    def one(f, _):
        packet_ref[f, 0:16, :] = s_ref[f, pl.ds(pl.multiple_of(start, 16), 16), :]
        for h in range(2):
            held = jnp.zeros((8, width), jnp.float32)
            for a in range(depth):
                row = a * 16 + h * 8
                held = jnp.where(
                    pair == a, pltpu.roll(s_ref[f, row : row + 8, :], 2 * a + 1, 1), held
                )
            packet_ref[f, 16 + 8 * h : 24 + 8 * h, :] = held
        low_ref[f] = s_ref[f, pl.ds(0, depth, stride=16), :]
        high_ref[f] = s_ref[f, pl.ds(15, depth, stride=16), :]
        return 0

    lax.fori_loop(0, fields, one, 0)


def pack(info, state):
    fields, rows, width = state.shape
    row = jax.ShapeDtypeStruct((fields, rows // 16, width), jnp.float32)
    return pl.pallas_call(
        pack_kernel,
        out_shape=(jax.ShapeDtypeStruct((fields, 32, width), jnp.float32), row, row),
        in_specs=[SMEM, VMEM],
        out_specs=(VMEM, VMEM, VMEM),
        compiler_params=params(),
        name="pack",
    )(info, state)


def relay_kernel(info, partner, ids_ref, shares_ref, *refs):
    packets, outs, table = refs[:8], refs[8:12], refs[12]
    fields, _, width = packets[0].shape
    own = info[0]
    sources = [own ^ k for k in SOURCES]
    dests = [own ^ k for k in DESTS]
    lane = lanes((8, width))
    turn = lax.broadcasted_iota(jnp.int32, (8, width), 0)
    tile = ((lane >> 4) - turn) & 7
    for d, dest in enumerate(dests):
        wanted = ids_ref[dest]
        share = shares_ref[dest]
        for q, source in enumerate(sources):
            there = tile + source * 8
            total = jnp.zeros((8, width), jnp.float32)
            for k in range(4):
                total = total + jnp.where(wanted[k : k + 1] == there, share[k : k + 1], 0.0)
            table[d, q] = total
    even = (lane & 1) == 0
    above = [[(partner[d] == q).astype(jnp.float32) for q in sources] for d in dests]
    below = [[(partner[q] == d).astype(jnp.float32) for q in sources] for d in dests]

    def one(i, _):
        f = i >> 1
        low = pl.multiple_of((i & 1) * 8, 8)
        high = pl.multiple_of(16 + (i & 1) * 8, 8)
        totals = [jnp.zeros((8, width), jnp.float32) for _ in dests]
        uppers = [jnp.zeros((8, width), jnp.float32) for _ in dests]
        lowers = [jnp.zeros((8, width), jnp.float32) for _ in dests]
        for q in range(8):
            face = packets[q][f, pl.ds(low, 8), :]
            edge = packets[q][f, pl.ds(high, 8), :]
            for t in range(8):
                turned = face if t == 0 else pltpu.roll(face, 16 * t, 1)
                for d in range(4):
                    totals[d] = totals[d] + turned * table[d, q, t : t + 1, :]
            for d in range(4):
                uppers[d] = uppers[d] + above[d][q] * edge
                lowers[d] = lowers[d] + below[d][q] * edge
        for d in range(4):
            outs[d][f, pl.ds(low, 8), :] = totals[d]
            outs[d][f, pl.ds(high, 8), :] = jnp.where(
                even, pltpu.roll(uppers[d], width - 1, 1), pltpu.roll(lowers[d], 1, 1)
            )
        return 0

    lax.fori_loop(0, fields * 2, one, 0)


def relay(info, partner, ids, shares, packets):
    shape = jax.ShapeDtypeStruct(packets[0].shape, jnp.float32)
    return pl.pallas_call(
        relay_kernel,
        out_shape=(shape,) * 4,
        in_specs=[SMEM, SMEM] + [VMEM] * 10,
        out_specs=(VMEM,) * 4,
        scratch_shapes=[pltpu.VMEM((4, 8, 8, 128), jnp.float32)],
        compiler_params=params(),
        name="relay",
    )(info, partner, ids, shares, *packets)


def stage_kernel(first, *refs):
    if first:
        (info, coupling, v_hbm, prior, older, axial, pitch, visc, inflow, halo_low, halo_high) = refs[:11]
        parts, (out, base, packet, low, high), (line, ghost, sem) = refs[11:15], refs[15:20], refs[20:]
    else:
        (info, coupling, v_hbm, base, axial, pitch, visc, inflow, halo_low, halo_high) = refs[:10]
        parts, (out,), (line, ghost, sem) = refs[10:14], refs[14:15], refs[15:]
    fields, rows, width = line.shape[0], line.shape[1] - 32, line.shape[2]
    depth = rows // 16
    step = pl.program_id(0)
    rotor = info[1] == 1

    @pl.when(step == 0)
    def _():
        copy = pltpu.make_async_copy(v_hbm, line.at[:, pl.ds(16, rows), :], sem)
        copy.start()
        for f in range(fields):
            ghost[f] = (parts[0][f] + parts[1][f]) + (parts[2][f] + parts[3][f])
        if first:
            packet[...] = jnp.zeros_like(packet)
        copy.wait()
        for f in range(fields):
            line[f, 0:16, :] = jnp.where(rotor, inflow[f], ghost[f, 0:16, :])
            line[f, rows + 16 : rows + 32, :] = jnp.where(
                rotor, ghost[f, 0:16, :], line[f, rows : rows + 16, :]
            )

    lane = lanes((8, width))
    sub = lax.broadcasted_iota(jnp.int32, (8, width), 0)
    head, tail = lane == 0, lane == width - 1
    top, bottom = sub == 0, sub == 7

    def one(j, _):
        a = step * LAYERS + j
        here = (a + 1) * 16
        back = lax.rem(width - 1 - 2 * a, width)
        coefs = []
        for h in range(2):
            speed = axial[j, 8 * h : 8 * h + 8, :]
            cross = pitch[j, 8 * h : 8 * h + 8, :]
            nu = visc[j, 8 * h : 8 * h + 8, :]
            dt = CFL / (speed + jnp.abs(cross) + 6.0 * nu + 1.5 / STEP_DT)
            spread = dt * nu
            half_axial = 0.5 * dt * speed
            half_pitch = 0.5 * dt * cross
            coefs.append(
                (
                    dt,
                    -(1.5 / STEP_DT) * dt - 6.0 * spread,
                    spread - half_axial,
                    spread + half_axial,
                    spread - half_pitch,
                    spread + half_pitch,
                    spread,
                )
            )

        def at(f, h, shift=0):
            return line[f, pl.ds(pl.multiple_of(here + 16 * shift + 8 * h, 8), 8), :]

        values = [[at(f, h) for h in range(2)] for f in range(fields)]
        for f in range(fields):
            x0, x1 = values[f]
            r0, r1 = pltpu.roll(x0, 1, 0), pltpu.roll(x1, 1, 0)
            d0, d1 = pltpu.roll(x0, 7, 0), pltpu.roll(x1, 7, 0)
            before = (jnp.where(top, halo_low[f, pl.ds(a, 1), :], r0), jnp.where(top, r0, r1))
            after = (jnp.where(bottom, d1, d0), jnp.where(bottom, halo_high[f, pl.ds(a, 1), :], d1))
            for h in range(2):
                dt, centre, forward, backward, right, left, spread = coefs[h]
                x = values[f][h]
                edge = pltpu.roll(ghost[f, 16 + 8 * h : 24 + 8 * h, :], back, 1)
                lower = jnp.where(head, edge, pltpu.roll(x, 1, 1))
                upper = jnp.where(tail, edge, pltpu.roll(x, width - 1, 1))
                mixed = coupling[f, 0] * values[0][h]
                for g in range(1, fields):
                    mixed = mixed + coupling[f, g] * values[g][h]
                change = (
                    (centre * x + spread * (before[h] + after[h]))
                    + (forward * at(f, h, 1) + backward * at(f, h, -1))
                    + (right * upper + left * lower)
                    - dt * mixed
                )
                place = (f, j, slice(8 * h, 8 * h + 8))
                if first:
                    known = dt * (prior[place] - 0.25 * older[place])
                    base[place] = known
                    moved = x + 0.5 * (known + change)
                    out[place] = moved
                    spot = (f, slice(16 + 8 * h, 24 + 8 * h))
                    packet[spot] = jnp.where(
                        (lane >> 1) == a, pltpu.roll(moved, 2 * a + 1, 1), packet[spot]
                    )
                    if h == 0:
                        low[f, pl.ds(j, 1), :] = moved[0:1]
                    else:
                        high[f, pl.ds(j, 1), :] = moved[7:8]
                else:
                    out[place] = x + (base[place] + change)
        return 0

    lax.fori_loop(0, LAYERS, one, 0)

    if first:
        face = info[1] * (depth - 1)

        @pl.when(step == face // LAYERS)
        def _():
            for f in range(fields):
                packet[f, 0:16, :] = out[f, lax.rem(face, LAYERS)]


def stage(first, info, coupling, v, given, speeds, inflow, halos, parts):
    fields, rows, width = v.shape
    depth = rows // 16
    whole = jax.ShapeDtypeStruct((fields, depth, 16, width), jnp.float32)
    block = pl.BlockSpec((fields, LAYERS, 16, width), lambda i: (0, i, 0, 0))
    cell = pl.BlockSpec((LAYERS, 16, width), lambda i: (i, 0, 0))
    line = pl.BlockSpec((fields, LAYERS, width), lambda i: (0, i, 0))
    packet_shape = parts[0].shape

    def fixed(shape):
        return pl.BlockSpec(shape, lambda i: (0,) * len(shape))

    packet = fixed(packet_shape)
    halo = fixed(halos[0].shape)
    out_shape, out_specs = [whole], [block]
    if first:
        edge = jax.ShapeDtypeStruct((fields, depth, width), jnp.float32)
        out_shape += [whole, jax.ShapeDtypeStruct(packet_shape, jnp.float32), edge, edge]
        out_specs += [block, packet, line, line]
    return pl.pallas_call(
        functools.partial(stage_kernel, first),
        grid=(depth // LAYERS,),
        out_shape=out_shape,
        in_specs=[SMEM, SMEM, pl.BlockSpec(memory_space=pl.ANY)]
        + [block] * len(given)
        + [cell] * 3
        + [fixed(inflow.shape), halo, halo]
        + [packet] * 4,
        out_specs=out_specs,
        scratch_shapes=[
            pltpu.VMEM((fields, rows + 32, width), jnp.float32),
            pltpu.VMEM(packet_shape, jnp.float32),
            pltpu.SemaphoreType.DMA(()),
        ],
        compiler_params=params(),
        name="first_stage" if first else "second_stage",
    )(info, coupling, v, *given, *speeds, inflow, *halos, *parts)


def flip(value, bits):
    return lax.ppermute(value, "passage", [(i, i ^ bits) for i in range(lax.axis_size("passage"))])


def spread(low, high):
    count = lax.axis_size("span")
    up = [(i, i + 1) for i in range(count - 1)]
    down = [(i + 1, i) for i in range(count - 1)]
    return lax.ppermute(high, "span", up), lax.ppermute(low, "span", down)


def on_device(
    state,
    previous,
    earlier,
    axial_speed,
    pitch_speed,
    viscosity,
    inflow,
    coupling,
    partner,
    tile_ids,
    tile_weights,
):
    own = lax.axis_index("passage")
    half = lax.axis_size("passage") // 2
    rotor = (own + (own >= half).astype(jnp.int32)) % 4 < 2
    info = jnp.stack([own, rotor.astype(jnp.int32)])
    fields, _, depth, spans, width = state.shape
    cells = state.reshape(fields, depth * spans, width)
    speeds = (axial_speed[0], pitch_speed[0], viscosity[0])
    weights = tile_weights.astype(jnp.float32)
    shares = weights / jnp.sum(weights, axis=2, keepdims=True)
    cut = width // tile_ids.shape[1]
    wide_ids = jnp.repeat(jnp.swapaxes(tile_ids, 1, 2), cut, axis=2)
    wide_shares = jnp.repeat(jnp.swapaxes(shares, 1, 2), cut, axis=2)

    def exchange(packet):
        near = [packet] + [flip(packet, k) for k in X_FLIPS]
        far = [flip(p, CORE_FLIP) for p in near]
        sent = relay(info, partner, wide_ids, wide_shares, near + far)
        return [sent[0]] + [flip(p, k) for p, k in zip(sent[1:], Z_FLIPS)]

    packet, low, high = pack(info, cells)
    parts = exchange(packet)
    halos = spread(low, high)
    middle, base, packet, low, high = stage(
        True, info, coupling, cells, (previous[:, 0], earlier[:, 0]), speeds, inflow, halos, parts
    )
    parts = exchange(packet)
    halos = spread(low, high)
    (updated,) = stage(
        False, info, coupling, middle.reshape(cells.shape), (base,), speeds, inflow, halos, parts
    )
    return updated[:, None]


def solution(mesh):
    placed = (
        P(None, "passage", None, "span", None),
        P(None, "passage", None, "span", None),
        P(None, "passage", None, "span", None),
        P("passage", None, "span", None),
        P("passage", None, "span", None),
        P("passage", None, "span", None),
        P(None, "span", None),
        P(),
        P(),
        P(),
        P(),
    )
    return jax.shard_map(
        on_device,
        mesh=mesh,
        in_specs=placed,
        out_specs=P(None, "passage", None, "span", None),
        check_vma=False,
    )
```

time: 366 us -> 95.3 us (0.26)
  the two profiles are of different devices: /device:TPU:1 before, /device:TPU:32 now
where the time goes in v1:
time: 95.3 us; the launch traced here: 93.8 us
  starting transfers between devices  40.9 us (43%)
  Pallas kernels  29 us (30%)
  waiting for transfers between devices  21.4 us (22%)
  local copies, waits for them, and re-layouts  2.07 us (2%)
    ppermute x20, starting transfers between devices, flip(): lax.ppermute(value, 'passage', [(i, i ^ bits) for i in range(lax.axis_siz...  25 us
    pallas_call x2, Pallas kernels, stage(): pl.pallas_call(functools.partial(stage_kernel, first), grid=(depth // LAY...  22 us
    ppermute x20, waiting for transfers between devices, flip(): lax.ppermute(value, 'passage', [(i, i ^ bits) for i in range(lax.axis_siz...  21.4 us
    ppermute x4, starting transfers between devices, spread(): return (lax.ppermute(high, 'span', up), lax.ppermute(low, 'span', down))  15.9 us
    pallas_call x2, Pallas kernels, relay(): pl.pallas_call(relay_kernel, out_shape=(shape,) * 4, in_specs=[SMEM, SMEM...  5.19 us
  transfers between devices with their start and end apart: 24, of which 12 were waited for; matrix products, arithmetic and copies ran while one was open for 0% of the time, Pallas kernels for 6%

profile of v1, /device:TPU:32, one launch (start us, length us, event | category | flops | bytes accessed | tf_op | source)
XLA Modules:
  0.0 93.8 jit_solution(14364420402321136333)
XLA Ops:
  0.0 0.1 pad_add_fusion.info.refs_0_
  0.1 1.8 %copy-done = f32[7,1,48,16,128]{4,3,2,1,0:T(8,128)S(1)} copy-done((f32[7,1,48,16,128]{4,3,2,1,0:T(8,128)S(1)}, f32[7,1,48,16,128]{4,3,2,1,0:T(8,128)}, u32[]{:S(2)}) %copy-start) | copy-done | bytes 2752536
  1.9 1.8 %pack.1 = (f32[7,32,128]{2,1,0:T(8,128)S(1)}, f32[7,48,128]{2,1,0:T(8,128)S(1)}, f32[7,48,128]{2,1,0:T(8,128)S(1)}) custom-call(s32[2]{0:T(128)S(1)} %pad_add_fusion.info.refs_0_, f32[7,768,128]{2,1,0:T(8,128)S(1)} %bitcast.18), custom_call_target="tpu_custom_call" | custom-call | tf_op jit(solution)/shard_map/pack/pallas_call | solution.py:59
  3.7 0.1 collective-permute-start.5
  3.8 2.8 %collective-permute-start.4 = (f32[7,32,128]{2,1,0:T(8,128)S(1)}, f32[7,32,128]{2,1,0:T(8,128)S(1)}, u32[]{:S(2)}, u32[]{:S(2)}) collective-permute-start(f32[7,32,128]{2,1,0:T(8,128)S(1)} %get-tuple-element.23.refs_0_), channel_id=1, source_target_pairs={{0,192},{8,200},{16,208},{24,216},{32,224},{40,232},{48,240},{56,2... | collective-permute-start | bytes 344072 | tf_op jit(solution)/shard_map/ppermute | solution.py:282
  6.7 0.8 collective-permute-start.3
  7.5 0.5 collective-permute-start.2
  8.0 3.5 %collective-permute-start = (f32[7,48,128]{2,1,0:T(8,128)S(1)}, f32[7,48,128]{2,1,0:T(8,128)S(1)}, u32[]{:S(2)}, u32[]{:S(2)}) collective-permute-start(f32[7,48,128]{2,1,0:T(8,128)S(1)} %get-tuple-element.21), channel_id=1, source_target_pairs={{0,1},{1,2},{2,3},{3,4},{4,5},{5,6},{6,7},{8,9},{9,10},{10,11},{11... | collective-permute-start | bytes 516104 | tf_op jit(solution)/shard_map/ppermute | solution.py:289
  11.5 0.0 collective-permute-done.5.refs_4_
  11.5 4.5 %collective-permute-start.1 = (f32[7,48,128]{2,1,0:T(8,128)S(1)}, f32[7,48,128]{2,1,0:T(8,128)S(1)}, u32[]{:S(2)}, u32[]{:S(2)}) collective-permute-start(f32[7,48,128]{2,1,0:T(8,128)S(1)} %get-tuple-element.22), channel_id=1, source_target_pairs={{1,0},{2,1},{3,2},{4,3},{5,4},{6,5},{7,6},{9,8},{10,9},{11,10},{12... | collective-permute-start | bytes 516104 | tf_op jit(solution)/shard_map/ppermute | solution.py:289
  16.0 0.0 collective-permute-done.4.refs_3_
  16.0 0.1 collective-permute-start.8
  16.1 0.0 collective-permute-done.3.refs_2_
  16.1 0.5 collective-permute-start.7
  16.6 0.0 collective-permute-done.2.refs_1_
  16.6 0.1 collective-permute-start.6
  16.8 0.1 copy.18.shares_ref
  16.9 0.1 copy.17.ids_ref
  17.0 0.4 collective-permute-done.8.refs_7_
  17.4 0.2 collective-permute-done.7.refs_6_
  17.6 0.4 collective-permute-done.6.refs_5_
  17.9 2.6 %relay.2 = (f32[7,32,128]{2,1,0:T(8,128)S(1)}, f32[7,32,128]{2,1,0:T(8,128)S(1)}, f32[7,32,128]{2,1,0:T(8,128)S(1)}, f32[7,32,128]{2,1,0:T(8,128)S(1)}) custom-call(s32[2]{0:T(128)S(1)} %pad_add_fusion.info.refs_0_, s32[32]{0:T(128)S(1)} %copy-done.6, s32[32,4,128]{2,1,0:T(4,128)S(1)} %copy.17.ids_ref, f32[32,4,128]{2,1,0:T(4,128)S(1)} %copy.18.shares_ref, ...), custom_call_target="tpu_custom_call" | custom-call | tf_op jit(solution)/shard_map/relay/pallas_call | solution.py:120
  20.5 3.4 %collective-permute-start.9 = (f32[7,32,128]{2,1,0:T(8,128)S(1)}, f32[7,32,128]{2,1,0:T(8,128)S(1)}, u32[]{:S(2)}, u32[]{:S(2)}) collective-permute-start(f32[7,32,128]{2,1,0:T(8,128)S(1)} %get-tuple-element.25), channel_id=1, source_target_pairs={{0,16},{8,24},{16,0},{24,8},{32,48},{40,56},{48,32},{56,40},{64,80... | collective-permute-start | bytes 344072 | tf_op jit(solution)/shard_map/ppermute | solution.py:282
  23.9 4.5 %collective-permute-start.10 = (f32[7,32,128]{2,1,0:T(8,128)S(1)}, f32[7,32,128]{2,1,0:T(8,128)S(1)}, u32[]{:S(2)}, u32[]{:S(2)}) collective-permute-start(f32[7,32,128]{2,1,0:T(8,128)S(1)} %get-tuple-element.26), channel_id=1, source_target_pairs={{0,32},{8,40},{16,48},{24,56},{32,0},{40,8},{48,16},{56,24},{64,96... | collective-permute-start | bytes 344072 | tf_op jit(solution)/shard_map/ppermute | solution.py:282
  28.4 0.0 collective-permute-done.1.refs_10_
  28.4 3.2 %collective-permute-done.9.refs_12_ = f32[7,32,128]{2,1,0:T(8,128)S(1)} collective-permute-done((f32[7,32,128]{2,1,0:T(8,128)S(1)}, f32[7,32,128]{2,1,0:T(8,128)S(1)}, u32[]{:S(2)}, u32[]{:S(2)}) %collective-permute-start.9) | collective-permute-done | bytes 114720 | tf_op jit(solution)/shard_map/ppermute | solution.py:282
  31.6 1.3 %collective-permute-done.10.refs_13_ = f32[7,32,128]{2,1,0:T(8,128)S(1)} collective-permute-done((f32[7,32,128]{2,1,0:T(8,128)S(1)}, f32[7,32,128]{2,1,0:T(8,128)S(1)}, u32[]{:S(2)}, u32[]{:S(2)}) %collective-permute-start.10) | collective-permute-done | bytes 114720 | tf_op jit(solution)/shard_map/ppermute | solution.py:282
  32.9 4.0 %collective-permute-done.11.refs_14_ = f32[7,32,128]{2,1,0:T(8,128)S(1)} collective-permute-done((f32[7,32,128]{2,1,0:T(8,128)S(1)}, f32[7,32,128]{2,1,0:T(8,128)S(1)}, u32[]{:S(2)}, u32[]{:S(2)}) %collective-permute-start.11) | collective-permute-done | bytes 114720 | tf_op jit(solution)/shard_map/ppermute | solution.py:282
  36.9 13.6 %first_stage.1 = (f32[7,48,16,128]{3,2,1,0:T(8,128)S(1)}, f32[7,48,16,128]{3,2,1,0:T(8,128)}, f32[7,32,128]{2,1,0:T(8,128)S(1)}, f32[7,48,128]{2,1,0:T(8,128)S(1)}, f32[7,48,128]{2,1,0:T(8,128)S(1)}) custom-call(s32[2]{0:T(128)S(1)} %pad_add_fusion.info.refs_0_, f32[7,7]{1,0:T(8,128)S(1)} %copy-done.5, f32[7,768,128]{2,1,0:T(8,128)} %bitcast.17, ...), custom_call_target="tpu_custom_call" | custom-call | tf_op jit(solution)/shard_map/first_stage/pallas_call | solution.py:261
  50.5 1.8 %collective-permute-start.16 = (f32[7,32,128]{2,1,0:T(8,128)S(1)}, f32[7,32,128]{2,1,0:T(8,128)S(1)}, u32[]{:S(2)}, u32[]{:S(2)}) collective-permute-start(f32[7,32,128]{2,1,0:T(8,128)S(1)} %get-tuple-element.32.refs_0_), channel_id=1, source_target_pairs={{0,192},{8,200},{16,208},{24,216},{32,224},{40,232},{48,240},{56,2... | collective-permute-start | bytes 344072 | tf_op jit(solution)/shard_map/ppermute | solution.py:282
  52.4 0.8 collective-permute-start.15
  53.2 1.5 %collective-permute-start.14 = (f32[7,32,128]{2,1,0:T(8,128)S(1)}, f32[7,32,128]{2,1,0:T(8,128)S(1)}, u32[]{:S(2)}, u32[]{:S(2)}) collective-permute-start(f32[7,32,128]{2,1,0:T(8,128)S(1)} %get-tuple-element.32.refs_0_), channel_id=1, source_target_pairs={{0,64},{8,72},{16,80},{24,88},{32,96},{40,104},{48,112},{56,120},{... | collective-permute-start | bytes 344072 | tf_op jit(solution)/shard_map/ppermute | solution.py:282
  54.7 4.0 %collective-permute-done.16.refs_3_ = f32[7,32,128]{2,1,0:T(8,128)S(1)} collective-permute-done((f32[7,32,128]{2,1,0:T(8,128)S(1)}, f32[7,32,128]{2,1,0:T(8,128)S(1)}, u32[]{:S(2)}, u32[]{:S(2)}) %collective-permute-start.16) | collective-permute-done | bytes 114720 | tf_op jit(solution)/shard_map/ppermute | solution.py:282
  58.7 0.7 collective-permute-done.15.refs_2_
  59.4 0.0 collective-permute-start.19
  59.4 0.6 collective-permute-done.14.refs_1_
  60.0 5.0 %collective-permute-start.12 = (f32[7,48,128]{2,1,0:T(8,128)S(1)}, f32[7,48,128]{2,1,0:T(8,128)S(1)}, u32[]{:S(2)}, u32[]{:S(2)}) collective-permute-start(f32[7,48,128]{2,1,0:T(8,128)S(1)} %get-tuple-element.30), channel_id=1, source_target_pairs={{0,1},{1,2},{2,3},{3,4},{4,5},{5,6},{6,7},{8,9},{9,10},{10,11},{11... | collective-permute-start | bytes 516104 | tf_op jit(solution)/shard_map/ppermute | solution.py:289
  65.0 2.9 %collective-permute-start.13 = (f32[7,48,128]{2,1,0:T(8,128)S(1)}, f32[7,48,128]{2,1,0:T(8,128)S(1)}, u32[]{:S(2)}, u32[]{:S(2)}) collective-permute-start(f32[7,48,128]{2,1,0:T(8,128)S(1)} %get-tuple-element.31), channel_id=1, source_target_pairs={{1,0},{2,1},{3,2},{4,3},{5,4},{6,5},{7,6},{9,8},{10,9},{11,10},{12... | collective-permute-start | bytes 516104 | tf_op jit(solution)/shard_map/ppermute | solution.py:289
  67.9 0.0 collective-permute-done.20.refs_7_
  68.0 0.0 collective-permute-done.19.refs_6_
  68.0 2.6 %relay.3 = (f32[7,32,128]{2,1,0:T(8,128)S(1)}, f32[7,32,128]{2,1,0:T(8,128)S(1)}, f32[7,32,128]{2,1,0:T(8,128)S(1)}, f32[7,32,128]{2,1,0:T(8,128)S(1)}) custom-call(s32[2]{0:T(128)S(1)} %pad_add_fusion.info.refs_0_, s32[32]{0:T(128)S(1)} %copy-done.6, s32[32,4,128]{2,1,0:T(4,128)S(1)} %copy.17.ids_ref, f32[32,4,128]{2,1,0:T(4,128)S(1)} %copy.18.shares_ref, ...), custom_call_target="tpu_custom_call" | custom-call | tf_op jit(solution)/shard_map/relay/pallas_call | solution.py:120
  70.6 4.3 %collective-permute-start.21 = (f32[7,32,128]{2,1,0:T(8,128)S(1)}, f32[7,32,128]{2,1,0:T(8,128)S(1)}, u32[]{:S(2)}, u32[]{:S(2)}) collective-permute-start(f32[7,32,128]{2,1,0:T(8,128)S(1)} %get-tuple-element.34), channel_id=1, source_target_pairs={{0,16},{8,24},{16,0},{24,8},{32,48},{40,56},{48,32},{56,40},{64,80... | collective-permute-start | bytes 344072 | tf_op jit(solution)/shard_map/ppermute | solution.py:282
  74.9 2.3 %collective-permute-start.22 = (f32[7,32,128]{2,1,0:T(8,128)S(1)}, f32[7,32,128]{2,1,0:T(8,128)S(1)}, u32[]{:S(2)}, u32[]{:S(2)}) collective-permute-start(f32[7,32,128]{2,1,0:T(8,128)S(1)} %get-tuple-element.35), channel_id=1, source_target_pairs={{0,32},{8,40},{16,48},{24,56},{32,0},{40,8},{48,16},{56,24},{64,96... | collective-permute-start | bytes 344072 | tf_op jit(solution)/shard_map/ppermute | solution.py:282
  77.2 1.4 %collective-permute-start.23 = (f32[7,32,128]{2,1,0:T(8,128)S(1)}, f32[7,32,128]{2,1,0:T(8,128)S(1)}, u32[]{:S(2)}, u32[]{:S(2)}) collective-permute-start(f32[7,32,128]{2,1,0:T(8,128)S(1)} %get-tuple-element.36), channel_id=1, source_target_pairs={{0,48},{8,56},{16,32},{24,40},{32,16},{40,24},{48,0},{56,8},{64,11... | collective-permute-start | bytes 344072 | tf_op jit(solution)/shard_map/ppermute | solution.py:282
  78.6 4.8 %collective-permute-done.21.refs_11_ = f32[7,32,128]{2,1,0:T(8,128)S(1)} collective-permute-done((f32[7,32,128]{2,1,0:T(8,128)S(1)}, f32[7,32,128]{2,1,0:T(8,128)S(1)}, u32[]{:S(2)}, u32[]{:S(2)}) %collective-permute-start.21) | collective-permute-done | bytes 114720 | tf_op jit(solution)/shard_map/ppermute | solution.py:282
  83.4 1.7 %collective-permute-done.22.refs_12_ = f32[7,32,128]{2,1,0:T(8,128)S(1)} collective-permute-done((f32[7,32,128]{2,1,0:T(8,128)S(1)}, f32[7,32,128]{2,1,0:T(8,128)S(1)}, u32[]{:S(2)}, u32[]{:S(2)}) %collective-permute-start.22) | collective-permute-done | bytes 114720 | tf_op jit(solution)/shard_map/ppermute | solution.py:282
  85.2 0.1 collective-permute-done.23.refs_13_
  85.3 8.5 %second_stage.1 = f32[7,48,16,128]{3,2,1,0:T(8,128)} custom-call(s32[2]{0:T(128)S(1)} %pad_add_fusion.info.refs_0_, f32[7,7]{1,0:T(8,128)S(1)} %copy-done.5, f32[7,768,128]{2,1,0:T(8,128)S(1)} %bitcast.19, f32[7,48,16,128]{3,2,1,0:T(8,128)} %get-tuple-element.29.refs_3_, f32[48,16,128]{2,1,0:T(8,128)S(1)} %bitcast.21, f32[48,16,128]{2,1,0:T(8,128)S(1)} %bitcast.23, ...), custom_call_target="tpu_custom_call" | custom-call | tf_op jit(solution)/shard_map/second_stage/pallas_call | solution.py:261
  (31 shorter events, 0.1 us)
Async XLA Ops:
  0.0 16.7 %copy-start.8 = (s32[32,8,4]{0,2,1:T(4,128)S(1)}, s32[32,8,4]{0,2,1:T(4,128)}, u32[]{:S(2)}) copy-start(s32[32,8,4]{0,2,1:T(4,128)} %param.21) | copy-start | bytes 12292
  0.0 16.7 %copy-start.7 = (s32[32,8,4]{0,2,1:T(4,128)S(1)}, s32[32,8,4]{0,2,1:T(4,128)}, u32[]{:S(2)}) copy-start(s32[32,8,4]{0,2,1:T(4,128)} %param.20) | copy-start | bytes 12292
  0.0 17.9 %copy-start.6 = (s32[32]{0:T(128)S(1)}, s32[32]{0:T(128)}, u32[]{:S(2)}) copy-start(s32[32]{0:T(128)} %partner.3) | copy-start | bytes 388
  0.0 36.9 %copy-start.5 = (f32[7,7]{1,0:T(8,128)S(1)}, f32[7,7]{1,0:T(8,128)}, u32[]{:S(2)}) copy-start(f32[7,7]{1,0:T(8,128)} %refs_1_.3) | copy-start | bytes 592
  0.1 1.8 %copy-start = (f32[7,1,48,16,128]{4,3,2,1,0:T(8,128)S(1)}, f32[7,1,48,16,128]{4,3,2,1,0:T(8,128)}, u32[]{:S(2)}) copy-start(f32[7,1,48,16,128]{4,3,2,1,0:T(8,128)} %param.11) | copy-start | bytes 8257540
  1.9 35.0 %copy-start.1 = (f32[1,48,16,128]{3,2,1,0:T(8,128)S(1)}, f32[1,48,16,128]{3,2,1,0:T(8,128)}, u32[]{:S(2)}) copy-start(f32[1,48,16,128]{3,2,1,0:T(8,128)} %param.14) | copy-start | bytes 1179652
  1.9 35.0 %copy-start.2 = (f32[1,48,16,128]{3,2,1,0:T(8,128)S(1)}, f32[1,48,16,128]{3,2,1,0:T(8,128)}, u32[]{:S(2)}) copy-start(f32[1,48,16,128]{3,2,1,0:T(8,128)} %param.15) | copy-start | bytes 1179652
  1.9 35.0 %copy-start.3 = (f32[1,48,16,128]{3,2,1,0:T(8,128)S(1)}, f32[1,48,16,128]{3,2,1,0:T(8,128)}, u32[]{:S(2)}) copy-start(f32[1,48,16,128]{3,2,1,0:T(8,128)} %param.16) | copy-start | bytes 1179652
  1.9 35.0 %copy-start.4 = (f32[7,16,128]{2,1,0:T(8,128)S(1)}, f32[7,16,128]{2,1,0:T(8,128)}, u32[]{:S(2)}) copy-start(f32[7,16,128]{2,1,0:T(8,128)} %refs_7_.1) | copy-start | bytes 172036
  3.7 7.8 %collective-permute-start.5 = (f32[7,32,128]{2,1,0:T(8,128)S(1)}, f32[7,32,128]{2,1,0:T(8,128)S(1)}, u32[]{:S(2)}, u32[]{:S(2)}) collective-permute-start(f32[7,32,128]{2,1,0:T(8,128)S(1)} %get-tuple-element.23.refs_0_), channel_id=1, source_target_pairs={{0,8},{8,0},{16,24},{24,16},{32,40},{40,32},{48,56},{56,48},{64,72... | collective-permute-start | bytes 344072 | tf_op jit(solution)/shard_map/ppermute | solution.py:282
  3.8 12.2 %collective-permute-start.4 = (f32[7,32,128]{2,1,0:T(8,128)S(1)}, f32[7,32,128]{2,1,0:T(8,128)S(1)}, u32[]{:S(2)}, u32[]{:S(2)}) collective-permute-start(f32[7,32,128]{2,1,0:T(8,128)S(1)} %get-tuple-element.23.refs_0_), channel_id=1, source_target_pairs={{0,192},{8,200},{16,208},{24,216},{32,224},{40,232},{48,240},{56,2... | collective-permute-start | bytes 344072 | tf_op jit(solution)/shard_map/ppermute | solution.py:282
  6.7 9.4 %collective-permute-start.3 = (f32[7,32,128]{2,1,0:T(8,128)S(1)}, f32[7,32,128]{2,1,0:T(8,128)S(1)}, u32[]{:S(2)}, u32[]{:S(2)}) collective-permute-start(f32[7,32,128]{2,1,0:T(8,128)S(1)} %get-tuple-element.23.refs_0_), channel_id=1, source_target_pairs={{0,128},{8,136},{16,144},{24,152},{32,160},{40,168},{48,176},{56,1... | collective-permute-start | bytes 344072 | tf_op jit(solution)/shard_map/ppermute | solution.py:282
  7.5 9.1 %collective-permute-start.2 = (f32[7,32,128]{2,1,0:T(8,128)S(1)}, f32[7,32,128]{2,1,0:T(8,128)S(1)}, u32[]{:S(2)}, u32[]{:S(2)}) collective-permute-start(f32[7,32,128]{2,1,0:T(8,128)S(1)} %get-tuple-element.23.refs_0_), channel_id=1, source_target_pairs={{0,64},{8,72},{16,80},{24,88},{32,96},{40,104},{48,112},{56,120},{... | collective-permute-start | bytes 344072 | tf_op jit(solution)/shard_map/ppermute | solution.py:282
  8.0 20.4 %collective-permute-start = (f32[7,48,128]{2,1,0:T(8,128)S(1)}, f32[7,48,128]{2,1,0:T(8,128)S(1)}, u32[]{:S(2)}, u32[]{:S(2)}) collective-permute-start(f32[7,48,128]{2,1,0:T(8,128)S(1)} %get-tuple-element.21), channel_id=1, source_target_pairs={{0,1},{1,2},{2,3},{3,4},{4,5},{5,6},{6,7},{8,9},{9,10},{10,11},{11... | collective-permute-start | bytes 516104 | tf_op jit(solution)/shard_map/ppermute | solution.py:289
  11.5 16.9 %collective-permute-start.1 = (f32[7,48,128]{2,1,0:T(8,128)S(1)}, f32[7,48,128]{2,1,0:T(8,128)S(1)}, u32[]{:S(2)}, u32[]{:S(2)}) collective-permute-start(f32[7,48,128]{2,1,0:T(8,128)S(1)} %get-tuple-element.22), channel_id=1, source_target_pairs={{1,0},{2,1},{3,2},{4,3},{5,4},{6,5},{7,6},{9,8},{10,9},{11,10},{12... | collective-permute-start | bytes 516104 | tf_op jit(solution)/shard_map/ppermute | solution.py:289
  16.0 1.4 %collective-permute-start.8 = (f32[7,32,128]{2,1,0:T(8,128)S(1)}, f32[7,32,128]{2,1,0:T(8,128)S(1)}, u32[]{:S(2)}, u32[]{:S(2)}) collective-permute-start(f32[7,32,128]{2,1,0:T(8,128)S(1)} %collective-permute-done.4.refs_3_), channel_id=1, source_target_pairs={{0,8},{8,0},{16,24},{24,16},{32,40},{40,32},{48,56},{56,48},{64,72... | collective-permute-start | bytes 344072 | tf_op jit(solution)/shard_map/ppermute | solution.py:282
  16.1 1.5 %collective-permute-start.7 = (f32[7,32,128]{2,1,0:T(8,128)S(1)}, f32[7,32,128]{2,1,0:T(8,128)S(1)}, u32[]{:S(2)}, u32[]{:S(2)}) collective-permute-start(f32[7,32,128]{2,1,0:T(8,128)S(1)} %collective-permute-done.3.refs_2_), channel_id=1, source_target_pairs={{0,8},{8,0},{16,24},{24,16},{32,40},{40,32},{48,56},{56,48},{64,72... | collective-permute-start | bytes 344072 | tf_op jit(solution)/shard_map/ppermute | solution.py:282
  16.6 1.3 %collective-permute-start.6 = (f32[7,32,128]{2,1,0:T(8,128)S(1)}, f32[7,32,128]{2,1,0:T(8,128)S(1)}, u32[]{:S(2)}, u32[]{:S(2)}) collective-permute-start(f32[7,32,128]{2,1,0:T(8,128)S(1)} %collective-permute-done.2.refs_1_), channel_id=1, source_target_pairs={{0,8},{8,0},{16,24},{24,16},{32,40},{40,32},{48,56},{56,48},{64,72... | collective-permute-start | bytes 344072 | tf_op jit(solution)/shard_map/ppermute | solution.py:282
  20.5 11.1 %collective-permute-start.9 = (f32[7,32,128]{2,1,0:T(8,128)S(1)}, f32[7,32,128]{2,1,0:T(8,128)S(1)}, u32[]{:S(2)}, u32[]{:S(2)}) collective-permute-start(f32[7,32,128]{2,1,0:T(8,128)S(1)} %get-tuple-element.25), channel_id=1, source_target_pairs={{0,16},{8,24},{16,0},{24,8},{32,48},{40,56},{48,32},{56,40},{64,80... | collective-permute-start | bytes 344072 | tf_op jit(solution)/shard_map/ppermute | solution.py:282
  23.9 9.0 %collective-permute-start.10 = (f32[7,32,128]{2,1,0:T(8,128)S(1)}, f32[7,32,128]{2,1,0:T(8,128)S(1)}, u32[]{:S(2)}, u32[]{:S(2)}) collective-permute-start(f32[7,32,128]{2,1,0:T(8,128)S(1)} %get-tuple-element.26), channel_id=1, source_target_pairs={{0,32},{8,40},{16,48},{24,56},{32,0},{40,8},{48,16},{56,24},{64,96... | collective-permute-start | bytes 344072 | tf_op jit(solution)/shard_map/ppermute | solution.py:282
  28.4 8.6 %collective-permute-start.11 = (f32[7,32,128]{2,1,0:T(8,128)S(1)}, f32[7,32,128]{2,1,0:T(8,128)S(1)}, u32[]{:S(2)}, u32[]{:S(2)}) collective-permute-start(f32[7,32,128]{2,1,0:T(8,128)S(1)} %get-tuple-element.27), channel_id=1, source_target_pairs={{0,48},{8,56},{16,32},{24,40},{32,16},{40,24},{48,0},{56,8},{64,11... | collective-permute-start | bytes 344072 | tf_op jit(solution)/shard_map/ppermute | solution.py:282
  50.5 8.2 %collective-permute-start.16 = (f32[7,32,128]{2,1,0:T(8,128)S(1)}, f32[7,32,128]{2,1,0:T(8,128)S(1)}, u32[]{:S(2)}, u32[]{:S(2)}) collective-permute-start(f32[7,32,128]{2,1,0:T(8,128)S(1)} %get-tuple-element.32.refs_0_), channel_id=1, source_target_pairs={{0,192},{8,200},{16,208},{24,216},{32,224},{40,232},{48,240},{56,2... | collective-permute-start | bytes 344072 | tf_op jit(solution)/shard_map/ppermute | solution.py:282
  52.4 7.0 %collective-permute-start.15 = (f32[7,32,128]{2,1,0:T(8,128)S(1)}, f32[7,32,128]{2,1,0:T(8,128)S(1)}, u32[]{:S(2)}, u32[]{:S(2)}) collective-permute-start(f32[7,32,128]{2,1,0:T(8,128)S(1)} %get-tuple-element.32.refs_0_), channel_id=1, source_target_pairs={{0,128},{8,136},{16,144},{24,152},{32,160},{40,168},{48,176},{56,1... | collective-permute-start | bytes 344072 | tf_op jit(solution)/shard_map/ppermute | solution.py:282
  53.2 6.7 %collective-permute-start.14 = (f32[7,32,128]{2,1,0:T(8,128)S(1)}, f32[7,32,128]{2,1,0:T(8,128)S(1)}, u32[]{:S(2)}, u32[]{:S(2)}) collective-permute-start(f32[7,32,128]{2,1,0:T(8,128)S(1)} %get-tuple-element.32.refs_0_), channel_id=1, source_target_pairs={{0,64},{8,72},{16,80},{24,88},{32,96},{40,104},{48,112},{56,120},{... | collective-permute-start | bytes 344072 | tf_op jit(solution)/shard_map/ppermute | solution.py:282
  54.7 10.3 %collective-permute-start.17 = (f32[7,32,128]{2,1,0:T(8,128)S(1)}, f32[7,32,128]{2,1,0:T(8,128)S(1)}, u32[]{:S(2)}, u32[]{:S(2)}) collective-permute-start(f32[7,32,128]{2,1,0:T(8,128)S(1)} %get-tuple-element.32.refs_0_), channel_id=1, source_target_pairs={{0,8},{8,0},{16,24},{24,16},{32,40},{40,32},{48,56},{56,48},{64,72... | collective-permute-start | bytes 344072 | tf_op jit(solution)/shard_map/ppermute | solution.py:282
  58.7 9.2 %collective-permute-start.20 = (f32[7,32,128]{2,1,0:T(8,128)S(1)}, f32[7,32,128]{2,1,0:T(8,128)S(1)}, u32[]{:S(2)}, u32[]{:S(2)}) collective-permute-start(f32[7,32,128]{2,1,0:T(8,128)S(1)} %collective-permute-done.16.refs_3_), channel_id=1, source_target_pairs={{0,8},{8,0},{16,24},{24,16},{32,40},{40,32},{48,56},{56,48},{64,72... | collective-permute-start | bytes 344072 | tf_op jit(solution)/shard_map/ppermute | solution.py:282
  59.4 8.5 %collective-permute-start.19 = (f32[7,32,128]{2,1,0:T(8,128)S(1)}, f32[7,32,128]{2,1,0:T(8,128)S(1)}, u32[]{:S(2)}, u32[]{:S(2)}) collective-permute-start(f32[7,32,128]{2,1,0:T(8,128)S(1)} %collective-permute-done.15.refs_2_), channel_id=1, source_target_pairs={{0,8},{8,0},{16,24},{24,16},{32,40},{40,32},{48,56},{56,48},{64,72... | collective-permute-start | bytes 344072 | tf_op jit(solution)/shard_map/ppermute | solution.py:282
  60.0 8.0 %collective-permute-start.18 = (f32[7,32,128]{2,1,0:T(8,128)S(1)}, f32[7,32,128]{2,1,0:T(8,128)S(1)}, u32[]{:S(2)}, u32[]{:S(2)}) collective-permute-start(f32[7,32,128]{2,1,0:T(8,128)S(1)} %collective-permute-done.14.refs_1_), channel_id=1, source_target_pairs={{0,8},{8,0},{16,24},{24,16},{32,40},{40,32},{48,56},{56,48},{64,72... | collective-permute-start | bytes 344072 | tf_op jit(solution)/shard_map/ppermute | solution.py:282
  60.0 18.6 %collective-permute-start.12 = (f32[7,48,128]{2,1,0:T(8,128)S(1)}, f32[7,48,128]{2,1,0:T(8,128)S(1)}, u32[]{:S(2)}, u32[]{:S(2)}) collective-permute-start(f32[7,48,128]{2,1,0:T(8,128)S(1)} %get-tuple-element.30), channel_id=1, source_target_pairs={{0,1},{1,2},{2,3},{3,4},{4,5},{5,6},{6,7},{8,9},{9,10},{10,11},{11... | collective-permute-start | bytes 516104 | tf_op jit(solution)/shard_map/ppermute | solution.py:289
  65.0 13.6 %collective-permute-start.13 = (f32[7,48,128]{2,1,0:T(8,128)S(1)}, f32[7,48,128]{2,1,0:T(8,128)S(1)}, u32[]{:S(2)}, u32[]{:S(2)}) collective-permute-start(f32[7,48,128]{2,1,0:T(8,128)S(1)} %get-tuple-element.31), channel_id=1, source_target_pairs={{1,0},{2,1},{3,2},{4,3},{5,4},{6,5},{7,6},{9,8},{10,9},{11,10},{12... | collective-permute-start | bytes 516104 | tf_op jit(solution)/shard_map/ppermute | solution.py:289
  70.6 12.8 %collective-permute-start.21 = (f32[7,32,128]{2,1,0:T(8,128)S(1)}, f32[7,32,128]{2,1,0:T(8,128)S(1)}, u32[]{:S(2)}, u32[]{:S(2)}) collective-permute-start(f32[7,32,128]{2,1,0:T(8,128)S(1)} %get-tuple-element.34), channel_id=1, source_target_pairs={{0,16},{8,24},{16,0},{24,8},{32,48},{40,56},{48,32},{56,40},{64,80... | collective-permute-start | bytes 344072 | tf_op jit(solution)/shard_map/ppermute | solution.py:282
  74.9 10.2 %collective-permute-start.22 = (f32[7,32,128]{2,1,0:T(8,128)S(1)}, f32[7,32,128]{2,1,0:T(8,128)S(1)}, u32[]{:S(2)}, u32[]{:S(2)}) collective-permute-start(f32[7,32,128]{2,1,0:T(8,128)S(1)} %get-tuple-element.35), channel_id=1, source_target_pairs={{0,32},{8,40},{16,48},{24,56},{32,0},{40,8},{48,16},{56,24},{64,96... | collective-permute-start | bytes 344072 | tf_op jit(solution)/shard_map/ppermute | solution.py:282
  77.2 8.1 %collective-permute-start.23 = (f32[7,32,128]{2,1,0:T(8,128)S(1)}, f32[7,32,128]{2,1,0:T(8,128)S(1)}, u32[]{:S(2)}, u32[]{:S(2)}) collective-permute-start(f32[7,32,128]{2,1,0:T(8,128)S(1)} %get-tuple-element.36), channel_id=1, source_target_pairs={{0,48},{8,56},{16,32},{24,40},{32,16},{40,24},{48,0},{56,8},{64,11... | collective-permute-start | bytes 344072 | tf_op jit(solution)/shard_map/ppermute | solution.py:282

commit v2 on v1

v2 whole, which is shorter than its diff:
```python
import functools

import jax
import jax.numpy as jnp
from jax import lax
from jax.experimental import pallas as pl
from jax.experimental.pallas import tpu as pltpu
from jax.sharding import PartitionSpec as P

CFL = 0.8
STEP_DT = 2.0

X_FLIPS = (8, 16, 24)
Z_FLIPS = (2, 4, 6)
CORE_FLIP = 1
SOURCES = (0, 8, 16, 24, 1, 9, 17, 25)

LAYERS = 8
UNITS = 14
EDGE = UNITS * 8
DEPTH = 48
TIGHT = 11

SMEM = pl.BlockSpec(memory_space=pltpu.SMEM)
VMEM = pl.BlockSpec(memory_space=pltpu.VMEM)
ANY = pl.BlockSpec(memory_space=pl.ANY)


def params(mib):
    return pltpu.CompilerParams(vmem_limit_bytes=mib * 1024 * 1024)


def lanes(shape=(8, 128)):
    return lax.broadcasted_iota(jnp.int32, shape, len(shape) - 1)


def struct(*shape):
    return jax.ShapeDtypeStruct(shape, jnp.float32)


def fixed(*shape):
    return pl.BlockSpec(shape, lambda i: (0,) * len(shape))


def unit(ref, u):
    return ref[8 * u : 8 * u + 8, :]


def tighten(units):
    lane = lanes()
    packed = []
    for first in range(0, 12, 4):
        for j in range(3):
            spare = pltpu.roll(units[first + 3], 96 - 32 * j, 1)
            packed.append(jnp.where(lane < 96, units[first + j], spare))
    return packed + list(units[12:])


def loosen(packed):
    lane = lanes()
    units = []
    for first in range(0, 9, 3):
        a, b, c = packed[first : first + 3]
        last = jnp.where(
            lane < 32,
            pltpu.roll(a, 32, 1),
            jnp.where(lane < 64, pltpu.roll(b, 64, 1), pltpu.roll(c, 96, 1)),
        )
        units += [a, b, c, last]
    return units + list(packed[9:])


def is_rotor(passage):
    return ((passage + (passage >= 16).astype(jnp.int32)) & 3) < 2


def summed(parts, u):
    return (unit(parts[0], u) + unit(parts[1], u)) + (unit(parts[2], u) + unit(parts[3], u))


def chunk_copy(source, target, sem, c, base=0):
    rows = LAYERS * 16
    here = pl.multiple_of(c * rows, rows)
    there = pl.multiple_of(here + base, 16)
    return pltpu.make_async_copy(
        source.at[:, pl.ds(here, rows), :], target.at[:, pl.ds(there, rows), :], sem.at[c]
    )


def add_terms(info, ref, base, c, edge_add, face_add):
    fields, width = ref.shape[0], ref.shape[2]
    side = info[1] * (DEPTH - 1)
    lane = lanes()
    ends = (lane == 0) | (lane == width - 1)
    start = base + c * (LAYERS * 16)
    back = lax.rem(width - 2 * LAYERS * (DEPTH // LAYERS - 1 - c), width)

    def one(f, _):
        for h in range(2):
            turned = pltpu.roll(edge_add[pl.ds(pl.multiple_of(f * 16 + 8 * h, 8), 8), :], back, 1)
            for j in range(LAYERS):
                rows = pl.ds(pl.multiple_of(start + 16 * j + 8 * h, 8), 8)
                here = pltpu.roll(turned, width - 1 - 2 * (LAYERS - 1 - j), 1)
                ref[f, rows, :] = ref[f, rows, :] + jnp.where(ends, here, 0.0)
        return 0

    lax.fori_loop(0, fields, one, 0, unroll=True)

    @pl.when(side // LAYERS == c)
    def _():
        rows = pl.ds(pl.multiple_of(base + side * 16, 16), 16)
        for f in range(fields):
            ref[f, rows, :] = ref[f, rows, :] + face_add[16 * f : 16 * f + 16, :]


def pack_kernel(info, s_hbm, packet, low, high, units, s_ref, sem):
    fields, rows, width = s_ref.shape
    copies = [pltpu.make_async_copy(s_hbm.at[f], s_ref.at[f], sem.at[f]) for f in range(fields)]
    for copy in copies:
        copy.start()
    depth = rows // 16
    pair = lanes() >> 1
    start = info[1] * (rows - 16)

    def one(f, _):
        pltpu.make_async_copy(s_hbm.at[f], s_ref.at[f], sem.at[f]).wait()
        row = pl.multiple_of(f * 16, 16)
        packet[pl.ds(row, 16), :] = s_ref[f, pl.ds(pl.multiple_of(start, 16), 16), :]
        for h in range(2):
            held = jnp.zeros((8, width), jnp.float32)
            for a in range(depth):
                at = a * 16 + h * 8
                p = depth - 1 - a
                held = jnp.where(pair == p, pltpu.roll(s_ref[f, at : at + 8, :], 2 * p + 1, 1), held)
            units[pl.ds(row + 8 * h, 8), :] = held
        low[f] = s_ref[f, pl.ds(0, depth, stride=16), :]
        high[f] = s_ref[f, pl.ds(15, depth, stride=16), :]
        return 0

    lax.fori_loop(0, fields, one, 0)
    for i, value in enumerate(tighten([unit(units, u) for u in range(UNITS)])):
        packet[EDGE + 8 * i : EDGE + 8 * i + 8, :] = value


def pack(info, cells):
    fields, rows, width = cells.shape
    row = struct(fields, rows // 16, width)
    return pl.pallas_call(
        pack_kernel,
        out_shape=(struct(EDGE + 8 * TIGHT, width), row, row),
        in_specs=[SMEM, ANY],
        out_specs=(VMEM, VMEM, VMEM),
        scratch_shapes=[
            pltpu.VMEM((EDGE, width), jnp.float32),
            pltpu.VMEM(cells.shape, jnp.float32),
            pltpu.SemaphoreType.DMA((fields,)),
        ],
        compiler_params=params(48),
        name="pack",
    )(info, cells)


def relay_kernel(info, partner, ids_ref, shares_ref, *refs):
    packets, outs, (table, held) = refs[:8], refs[8:12], refs[12:]
    height, width = packets[0].shape
    own = info[0]
    lane = lanes()
    turn = lax.broadcasted_iota(jnp.int32, (8, width), 0)
    tile = ((lane >> 4) - turn) & 7
    even = (lane & 1) == 0
    held[...] = jnp.zeros_like(held)
    for q, bits in enumerate(SOURCES):
        source = own ^ bits
        other = (is_rotor(source) != is_rotor(own)).astype(jnp.int32)
        there = tile + source * 8
        for i in range(2):
            dest = own ^ (2 * (1 - other) + 4 * i)
            wanted, share = ids_ref[dest], shares_ref[dest]
            total = jnp.zeros((8, width), jnp.float32)
            for k in range(4):
                total = total + jnp.where(wanted[k : k + 1] == there, share[k : k + 1], 0.0)
            table[q, i] = total
    for q, bits in enumerate(SOURCES):
        source = own ^ bits
        other = (is_rotor(source) != is_rotor(own)).astype(jnp.int32)
        totals = [[jnp.zeros((8, width), jnp.float32)] * UNITS for _ in range(2)]
        for t in range(8):
            weights = [jnp.broadcast_to(table[q, i, t : t + 1, :], (8, width)) for i in range(2)]
            for u in range(UNITS):
                face = unit(packets[q], u)
                turned = face if t == 0 else pltpu.roll(face, 16 * t, 1)
                for i in range(2):
                    totals[i][u] = totals[i][u] + turned * weights[i]
        for i in range(2):
            for u in range(UNITS):
                rows = slice(8 * u, 8 * u + 8)
                held[1 - other, i, rows, :] = held[1 - other, i, rows, :] + totals[i][u]
        for i in range(2):
            dest = own ^ (2 * other + 4 * i)
            above = (partner[dest] == source).astype(jnp.float32)
            below = (partner[source] == dest).astype(jnp.float32)
            mask = jnp.where(even, below, above)
            for u in range(UNITS, UNITS + TIGHT):
                rows = slice(8 * u, 8 * u + 8)
                held[other, i, rows, :] = held[other, i, rows, :] + mask * unit(packets[q], u)
    for d in range(4):
        outs[d][0:EDGE, :] = held[d & 1, d >> 1, 0:EDGE, :]
        for u in range(UNITS, UNITS + TIGHT):
            rows = slice(8 * u, 8 * u + 8)
            edge = held[d & 1, d >> 1, rows, :]
            outs[d][rows, :] = jnp.where(even, pltpu.roll(edge, width - 1, 1), pltpu.roll(edge, 1, 1))


def relay(info, partner, ids, shares, packets):
    return pl.pallas_call(
        relay_kernel,
        out_shape=(struct(*packets[0].shape),) * 4,
        in_specs=[SMEM, SMEM] + [VMEM] * 10,
        out_specs=(VMEM,) * 4,
        scratch_shapes=[
            pltpu.VMEM((8, 2, 8, 128), jnp.float32),
            pltpu.VMEM((2, 2) + packets[0].shape, jnp.float32),
        ],
        compiler_params=params(48),
        name="relay",
    )(info, partner, ids, shares, *packets)


def interior_kernel(first, *refs):
    if first:
        info, coupling, v_hbm, prior, older, axial, pitch, visc, inflow, halo_low, halo_high, _ = refs[:12]
        (out, base, face, edges, edge_coef, face_coef, low, high) = refs[12:20]
        line, sem, ends = refs[20:]
    else:
        (info, coupling, v_hbm, base, axial, pitch, visc, inflow, halo_low, halo_high, _) = refs[:11]
        edge_add, face_add, out, line, sem = refs[11:]
    fields, rows, width = line.shape[0], line.shape[1] - 32, line.shape[2]
    depth = rows // 16
    step = pl.program_id(0)
    rotor = info[1] == 1
    side = info[1] * (depth - 1)

    chunks = depth // LAYERS

    def ready(c):
        chunk_copy(v_hbm, line, sem, c, 16).wait()
        if not first:
            add_terms(info, line, 16, c, edge_add, face_add)

        @pl.when(c == chunks - 1)
        def _():
            for f in range(fields):
                last = line[f, rows : rows + 16, :]
                line[f, rows + 16 : rows + 32, :] = jnp.where(rotor, 0.0, last)

    @pl.when(step == 0)
    def _():
        for c in range(chunks):
            chunk_copy(v_hbm, line, sem, c, 16).start()
        if first:
            edges[...] = jnp.zeros_like(edges)
            edge_coef[...] = jnp.zeros_like(edge_coef)
        for f in range(fields):
            line[f, 0:16, :] = jnp.where(rotor, inflow[f], 0.0)
        ready(0)

    @pl.when(step < chunks - 1)
    def _():
        ready(step + 1)

    lane = lanes()
    pair = lane >> 1
    sub = lax.broadcasted_iota(jnp.int32, (8, width), 0)
    head, tail = lane == 0, lane == width - 1
    top, bottom = sub == 0, sub == 7

    def one(j, _):
        a = step * LAYERS + j
        here = (a + 1) * 16
        coefs = []
        for h in range(2):
            speed = axial[j, 8 * h : 8 * h + 8, :]
            cross = pitch[j, 8 * h : 8 * h + 8, :]
            nu = visc[j, 8 * h : 8 * h + 8, :]
            dt = CFL / (speed + jnp.abs(cross) + 6.0 * nu + 1.5 / STEP_DT)
            even = dt * nu
            half_axial = 0.5 * dt * speed
            half_pitch = 0.5 * dt * cross
            forward, backward = even - half_axial, even + half_axial
            right, left = even - half_pitch, even + half_pitch
            centre = -(1.5 / STEP_DT) * dt - 6.0 * even
            if first:
                ends[j, 8 * h : 8 * h + 8, :] = jnp.where(tail, right, left)
            right, left = jnp.where(tail, 0.0, right), jnp.where(head, 0.0, left)
            coefs.append((dt, centre, forward, backward, right, left, even))

        def at(f, h, shift=0):
            return line[f, pl.ds(pl.multiple_of(here + 16 * shift + 8 * h, 8), 8), :]

        values = [[at(f, h) for h in range(2)] for f in range(fields)]
        for f in range(fields):
            x0, x1 = values[f]
            r0, r1 = pltpu.roll(x0, 1, 0), pltpu.roll(x1, 1, 0)
            d0, d1 = pltpu.roll(x0, 7, 0), pltpu.roll(x1, 7, 0)
            before = (jnp.where(top, halo_low[f, pl.ds(a, 1), :], r0), jnp.where(top, r0, r1))
            after = (jnp.where(bottom, d1, d0), jnp.where(bottom, halo_high[f, pl.ds(a, 1), :], d1))
            for h in range(2):
                dt, centre, forward, backward, right, left, even = coefs[h]
                x = values[f][h]
                mixed = coupling[f, 0] * values[0][h]
                for g in range(1, fields):
                    mixed = mixed + coupling[f, g] * values[g][h]
                change = (
                    (centre * x + even * (before[h] + after[h]))
                    + (forward * at(f, h, 1) + backward * at(f, h, -1))
                    + (right * pltpu.roll(x, width - 1, 1) + left * pltpu.roll(x, 1, 1))
                    - dt * mixed
                )
                place = (f, j, slice(8 * h, 8 * h + 8))
                if first:
                    known = dt * (prior[place] - 0.25 * older[place])
                    base[place] = known
                    moved = x + 0.5 * (known + change)
                    out[place] = moved
                    if h == 0:
                        low[f, pl.ds(j, 1), :] = moved[0:1]
                    else:
                        high[f, pl.ds(j, 1), :] = moved[7:8]
                else:
                    out[place] = x + (base[place] + change)
        return 0

    lax.fori_loop(0, LAYERS, one, 0, unroll=4)

    if first:

        def gather(target, rows, layer):
            part = jnp.zeros((8, width), jnp.float32)
            for j in range(LAYERS):
                p = LAYERS - 1 - j
                part = jnp.where(pair == p, pltpu.roll(layer(j), 2 * p + 1, 1), part)
            place = chunks - 1 - step
            part = pltpu.roll(part, 2 * LAYERS * place, 1)
            target[rows, :] = jnp.where(pair // LAYERS == place, part, target[rows, :])

        for h in range(2):
            rows_h = slice(8 * h, 8 * h + 8)
            gather(edge_coef, rows_h, lambda j: ends[j, rows_h, :])
            for f in range(fields):
                spot = slice(16 * f + 8 * h, 16 * f + 8 * h + 8)
                gather(edges, spot, lambda j: out[f, j, rows_h, :])

        @pl.when(step == side // LAYERS)
        def _():
            j = lax.rem(side, LAYERS)
            dt = CFL / (axial[j] + jnp.abs(pitch[j]) + 6.0 * visc[j] + 1.5 / STEP_DT)
            drift = 0.5 * axial[j]
            face_coef[...] = dt * (visc[j] + jnp.where(rotor, -drift, drift))
            for f in range(fields):
                face[16 * f : 16 * f + 16, :] = out[f, j]


def interior(first, info, coupling, v, given, speeds, inflow, halos, order, adds=()):
    fields, rows, width = v.shape
    depth = rows // 16
    whole = struct(fields, depth, 16, width)
    block = pl.BlockSpec((fields, LAYERS, 16, width), lambda i: (0, i, 0, 0))
    cell = pl.BlockSpec((LAYERS, 16, width), lambda i: (i, 0, 0))
    halo = fixed(*halos[0].shape)
    out_shape, out_specs = [whole], [block]
    if first:
        small = [(EDGE, width), (EDGE, width), (16, width), (16, width)]
        out_shape += [whole] + [struct(*s) for s in small]
        out_specs += [block] + [fixed(*s) for s in small]
        out_shape += [struct(fields, depth, width)] * 2
        out_specs += [pl.BlockSpec((fields, LAYERS, width), lambda i: (0, i, 0))] * 2
    return pl.pallas_call(
        functools.partial(interior_kernel, first),
        grid=(depth // LAYERS,),
        out_shape=out_shape,
        in_specs=[SMEM, SMEM, ANY]
        + [block] * len(given)
        + [cell] * 3
        + [fixed(*inflow.shape), halo, halo, ANY]
        + [fixed(*a.shape) for a in adds],
        out_specs=out_specs,
        scratch_shapes=[
            pltpu.VMEM((fields, rows + 32, width), jnp.float32),
            pltpu.SemaphoreType.DMA((depth // LAYERS,)),
        ]
        + [pltpu.VMEM((LAYERS, 16, width), jnp.float32)] * int(first),
        compiler_params=params(48),
        cost_estimate=pl.CostEstimate(flops=30_000_000, bytes_accessed=12_000_000, transcendentals=0),
        name="first_interior" if first else "second_interior",
    )(info, coupling, v, *given, *speeds, inflow, *halos, order, *adds)


def terms(scale, parts, edge_coef, face_coef):
    ghosts = loosen([summed(parts, UNITS + i) for i in range(TIGHT)])
    edge_terms = [scale * edge_coef[8 * (u & 1) : 8 * (u & 1) + 8, :] * ghosts[u] for u in range(UNITS)]
    face_terms = [
        scale * face_coef[8 * (u & 1) : 8 * (u & 1) + 8, :] * summed(parts, u) for u in range(UNITS)
    ]
    return edge_terms, face_terms


def boundary_kernel(info, *refs):
    parts, (face, edges, edge_coef, face_coef, low, high) = refs[:4], refs[4:10]
    packet, edge_add, face_add, new_low, new_high = refs[10:]
    width = face.shape[1]
    side = info[1] * (DEPTH - 1)
    lane = lanes()
    ends = (lane == 0) | (lane == width - 1)
    spot = DEPTH - 1 - side
    here = (lane >> 1) == spot
    layer = lax.broadcasted_iota(jnp.int32, (8, width), 0)
    edge_terms, face_terms = terms(0.5, parts, edge_coef, face_coef)
    packed = []
    for u in range(UNITS):
        rows = slice(8 * u, 8 * u + 8)
        edge_add[rows, :] = edge_terms[u]
        face_add[rows, :] = face_terms[u]
        turned = pltpu.roll(edge_terms[u], width - 1 - 2 * spot, 1)
        packet[rows, :] = unit(face, u) + face_terms[u] + jnp.where(ends, turned, 0.0)
        turned = pltpu.roll(face_terms[u], 2 * spot + 1, 1)
        packed.append(unit(edges, u) + edge_terms[u] + jnp.where(here, turned, 0.0))
    for i, value in enumerate(tighten(packed)):
        packet[EDGE + 8 * i : EDGE + 8 * i + 8, :] = value
    for old, new, last in ((low, new_low, 0), (high, new_high, 1)):
        row = 7 * last
        for f in range(UNITS // 2):
            edge = jnp.broadcast_to(edge_terms[2 * f + last][row : row + 1], (8, width))
            slid = jnp.broadcast_to(face_terms[2 * f + last][row : row + 1], (8, width))
            for a in range(0, DEPTH, 8):
                turned = pltpu.roll(edge, width + 1 - 2 * (DEPTH - a), 1, stride=2, stride_axis=0)
                added = jnp.where(ends, turned, 0.0) + jnp.where(layer + a == side, slid, 0.0)
                new[f, a : a + 8, :] = old[f, a : a + 8, :] + added


def boundary(info, parts, face, edges, edge_coef, face_coef, low, high):
    small, line = struct(*face.shape), struct(*low.shape)
    return pl.pallas_call(
        boundary_kernel,
        out_shape=(struct(*parts[0].shape), small, small, line, line),
        in_specs=[SMEM] + [VMEM] * 10,
        out_specs=(VMEM,) * 5,
        compiler_params=params(48),
        name="boundary",
    )(info, *parts, face, edges, edge_coef, face_coef, low, high)


def final_kernel(info, v, *refs):
    parts, (edge_coef, face_coef, out, held, edge_add, face_add, arrived, left) = refs[:4], refs[4:]
    chunks = DEPTH // LAYERS
    for c in range(chunks):
        chunk_copy(v, held, arrived, c).start()
    edge_terms, face_terms = terms(1.0, parts, edge_coef, face_coef)
    for u in range(UNITS):
        edge_add[8 * u : 8 * u + 8, :] = edge_terms[u]
        face_add[8 * u : 8 * u + 8, :] = face_terms[u]

    def one(c, _):
        chunk_copy(v, held, arrived, c).wait()
        add_terms(info, held, 0, c, edge_add, face_add)
        chunk_copy(held, out, left, c).start()
        return 0

    lax.fori_loop(0, chunks, one, 0)
    for c in range(chunks):
        chunk_copy(held, out, left, c).wait()


def correct_final(info, v, parts, edge_coef, face_coef):
    width = v.shape[2]
    return pl.pallas_call(
        final_kernel,
        out_shape=struct(*v.shape),
        in_specs=[SMEM, ANY] + [VMEM] * 6,
        out_specs=ANY,
        scratch_shapes=[pltpu.VMEM(v.shape, jnp.float32)]
        + [pltpu.VMEM((EDGE, width), jnp.float32)] * 2
        + [pltpu.SemaphoreType.DMA((DEPTH // LAYERS,))] * 2,
        compiler_params=params(48),
        name="correct_final",
    )(info, v, *parts, edge_coef, face_coef)


def flip(value, bits):
    return lax.ppermute(value, "passage", [(i, i ^ bits) for i in range(lax.axis_size("passage"))])


def span_halos(low, high):
    count = lax.axis_size("span")
    up = [(i, i + 1) for i in range(count - 1)]
    down = [(i + 1, i) for i in range(count - 1)]
    return lax.ppermute(high, "span", up), lax.ppermute(low, "span", down)


def on_device(
    state,
    previous,
    earlier,
    axial_speed,
    pitch_speed,
    viscosity,
    inflow,
    coupling,
    partner,
    tile_ids,
    tile_weights,
):
    own = lax.axis_index("passage")
    half = lax.axis_size("passage") // 2
    rotor = (own + (own >= half).astype(jnp.int32)) % 4 < 2
    info = jnp.stack([own, rotor.astype(jnp.int32)])
    fields, _, depth, spans, width = state.shape
    cells = state.reshape(fields, depth * spans, width)
    speeds = (axial_speed[0], pitch_speed[0], viscosity[0])
    weights = tile_weights.astype(jnp.float32)
    shares = weights / jnp.sum(weights, axis=2, keepdims=True)
    cut = width // tile_ids.shape[1]
    wide_ids = jnp.repeat(jnp.swapaxes(tile_ids, 1, 2), cut, axis=2)
    wide_shares = jnp.repeat(jnp.swapaxes(shares, 1, 2), cut, axis=2)

    def exchange(packet):
        near = [packet] + [flip(packet, k) for k in X_FLIPS]
        far = [flip(p, CORE_FLIP) for p in near]
        sent = relay(info, partner, wide_ids, wide_shares, near + far)
        return [sent[0]] + [flip(p, k) for p, k in zip(sent[1:], Z_FLIPS)]

    packet, low, high = pack(info, cells)
    parts = exchange(packet)
    halos = span_halos(low, high)
    middle, base, face, edges, edge_coef, face_coef, low, high = interior(
        True, info, coupling, cells, (previous[:, 0], earlier[:, 0]), speeds, inflow, halos, parts[0]
    )
    packet, edge_add, face_add, low, high = boundary(
        info, parts, face, edges, edge_coef, face_coef, low, high
    )
    halos = span_halos(low, high)
    parts = exchange(packet)
    (updated,) = interior(
        False,
        info,
        coupling,
        middle.reshape(cells.shape),
        (base,),
        speeds,
        inflow,
        halos,
        parts[0],
        (edge_add, face_add),
    )
    updated = correct_final(info, updated.reshape(cells.shape), parts, edge_coef, face_coef)
    return updated.reshape(state.shape)


def solution(mesh):
    placed = (
        P(None, "passage", None, "span", None),
        P(None, "passage", None, "span", None),
        P(None, "passage", None, "span", None),
        P("passage", None, "span", None),
        P("passage", None, "span", None),
        P("passage", None, "span", None),
        P(None, "span", None),
        P(),
        P(),
        P(),
        P(),
    )
    return jax.shard_map(
        on_device,
        mesh=mesh,
        in_specs=placed,
        out_specs=P(None, "passage", None, "span", None),
        check_vma=False,
    )
```

time: 95.3 us -> 80.7 us (0.85); the launches traced: 93.8 us -> 80.2 us
  waiting for transfers between devices: 21.4 us -> 6.25 us
  local copies, waits for them, and re-layouts: 2.07 us -> 3.57 us
    ppermute x20, waiting for transfers between devices: 21.4 us -> 6.24 us  [flip(): lax.ppermute(value, 'passage', [(i, i ^ bits) for i in range(lax.axis_siz...]
    unnamed x18 -> x20, local copies, waits for them, and re-layouts: 1.81 us -> 3.31 us
    pallas_call x5 -> x7, Pallas kernels: 29 us -> 29.8 us  [the longest x2 18.7 us: interior(): pl.pallas_call(functools.partial(interior_kernel, first), grid=(depth //...]
  transfers between devices with their start and end apart: 24 -> 24, of which waited for: 12 -> 5; matrix products, arithmetic and copies ran while one was open for 0% -> 0% of each run, Pallas kernels for 6% -> 28%
where the time goes in v2:
time: 80.7 us; the launch traced here: 80.2 us
  starting transfers between devices  40 us (50%)
  Pallas kernels  29.8 us (37%)
  waiting for transfers between devices  6.25 us (8%)
  local copies, waits for them, and re-layouts  3.57 us (4%)
    ppermute x20, starting transfers between devices, flip(): lax.ppermute(value, 'passage', [(i, i ^ bits) for i in range(lax.axis_siz...  24.1 us
    pallas_call x2, Pallas kernels, interior(): pl.pallas_call(functools.partial(interior_kernel, first), grid=(depth //...  18.7 us
    ppermute x4, starting transfers between devices, span_halos(): return (lax.ppermute(high, 'span', up), lax.ppermute(low, 'span', down))  15.9 us
    ppermute x20, waiting for transfers between devices, flip(): lax.ppermute(value, 'passage', [(i, i ^ bits) for i in range(lax.axis_siz...  6.24 us
    pallas_call x2, Pallas kernels, relay(): pl.pallas_call(relay_kernel, out_shape=(struct(*packets[0].shape),) * 4,...  3.69 us
    pallas_call x1, Pallas kernels, correct_final(): pl.pallas_call(final_kernel, out_shape=struct(*v.shape), in_specs=[SMEM,...  3.36 us
    unnamed x20, local copies, waits for them, and re-layouts  3.31 us
    pallas_call x1, Pallas kernels, pack(): pl.pallas_call(pack_kernel, out_shape=(struct(EDGE + 8 * TIGHT, width), r...  3.27 us
  transfers between devices with their start and end apart: 24, of which 5 were waited for; matrix products, arithmetic and copies ran while one was open for 0% of the time, Pallas kernels for 28%

profile of v2, /device:TPU:32, one launch (start us, length us, event | category | flops | bytes accessed | tf_op | source)
XLA Modules:
  0.0 80.2 jit_solution(11765308946905551268)
XLA Ops:
  0.0 0.1 pad_add_fusion.info.refs_0_
  0.1 1.8 %copy-done = f32[7,1,48,16,128]{4,3,2,1,0:T(8,128)S(1)} copy-done((f32[7,1,48,16,128]{4,3,2,1,0:T(8,128)S(1)}, f32[7,1,48,16,128]{4,3,2,1,0:T(8,128)}, u32[]{:S(2)}) %copy-start) | copy-done | bytes 2752536
  1.9 3.3 %pack.1 = (f32[200,128]{1,0:T(8,128)S(1)}, f32[7,48,128]{2,1,0:T(8,128)S(1)}, f32[7,48,128]{2,1,0:T(8,128)S(1)}) custom-call(s32[2]{0:T(128)S(1)} %pad_add_fusion.info.refs_0_, f32[7,768,128]{2,1,0:T(8,128)S(1)} %bitcast.20), custom_call_target="tpu_custom_call" | custom-call | tf_op jit(solution)/shard_map/pack/pallas_call | solution.py:148
  5.2 0.1 collective-permute-start.5
  5.3 2.8 %collective-permute-start.4 = (f32[200,128]{1,0:T(8,128)S(1)}, f32[200,128]{1,0:T(8,128)S(1)}, u32[]{:S(2)}, u32[]{:S(2)}) collective-permute-start(f32[200,128]{1,0:T(8,128)S(1)} %get-tuple-element.31.refs_0_), channel_id=1, source_target_pairs={{0,192},{8,200},{16,208},{24,216},{32,224},{40,232},{48,240},{56,2... | collective-permute-start | bytes 307208 | tf_op jit(solution)/shard_map/ppermute | solution.py:489
  8.1 0.8 collective-permute-start.3
  8.9 0.5 collective-permute-start.2
  9.5 3.5 %collective-permute-start = (f32[7,48,128]{2,1,0:T(8,128)S(1)}, f32[7,48,128]{2,1,0:T(8,128)S(1)}, u32[]{:S(2)}, u32[]{:S(2)}) collective-permute-start(f32[7,48,128]{2,1,0:T(8,128)S(1)} %get-tuple-element.29), channel_id=1, source_target_pairs={{0,1},{1,2},{2,3},{3,4},{4,5},{5,6},{6,7},{8,9},{9,10},{10,11},{11... | collective-permute-start | bytes 516104 | tf_op jit(solution)/shard_map/ppermute | solution.py:496
  12.9 0.0 collective-permute-done.5.refs_4_
  13.0 4.5 %collective-permute-start.1 = (f32[7,48,128]{2,1,0:T(8,128)S(1)}, f32[7,48,128]{2,1,0:T(8,128)S(1)}, u32[]{:S(2)}, u32[]{:S(2)}) collective-permute-start(f32[7,48,128]{2,1,0:T(8,128)S(1)} %get-tuple-element.30), channel_id=1, source_target_pairs={{1,0},{2,1},{3,2},{4,3},{5,4},{6,5},{7,6},{9,8},{10,9},{11,10},{12... | collective-permute-start | bytes 516104 | tf_op jit(solution)/shard_map/ppermute | solution.py:496
  17.4 0.1 collective-permute-start.8
  17.5 0.0 collective-permute-done.3.refs_2_
  17.5 0.5 collective-permute-start.7
  18.0 0.1 collective-permute-start.6
  18.2 0.1 copy.18.shares_ref
  18.4 0.1 copy.17.ids_ref
  18.5 0.3 collective-permute-done.8.refs_7_
  18.8 0.2 collective-permute-done.7.refs_6_
  19.0 0.4 collective-permute-done.6.refs_5_
  19.4 1.8 %relay.2 = (f32[200,128]{1,0:T(8,128)S(1)}, f32[200,128]{1,0:T(8,128)S(1)}, f32[200,128]{1,0:T(8,128)S(1)}, f32[200,128]{1,0:T(8,128)S(1)}) custom-call(s32[2]{0:T(128)S(1)} %pad_add_fusion.info.refs_0_, s32[32]{0:T(128)S(1)} %copy-done.7, s32[32,4,128]{2,1,0:T(4,128)S(1)} %copy.17.ids_ref, f32[32,4,128]{2,1,0:T(4,128)S(1)} %copy.18.shares_ref, ...), custom_call_target="tpu_custom_call" | custom-call | tf_op jit(solution)/shard_map/relay/pallas_call | solution.py:215
  21.2 3.4 %collective-permute-start.9 = (f32[200,128]{1,0:T(8,128)S(1)}, f32[200,128]{1,0:T(8,128)S(1)}, u32[]{:S(2)}, u32[]{:S(2)}) collective-permute-start(f32[200,128]{1,0:T(8,128)S(1)} %get-tuple-element.35), channel_id=1, source_target_pairs={{0,16},{8,24},{16,0},{24,8},{32,48},{40,56},{48,32},{56,40},{64,80... | collective-permute-start | bytes 307208 | tf_op jit(solution)/shard_map/ppermute | solution.py:489
  24.6 4.5 %collective-permute-start.10 = (f32[200,128]{1,0:T(8,128)S(1)}, f32[200,128]{1,0:T(8,128)S(1)}, u32[]{:S(2)}, u32[]{:S(2)}) collective-permute-start(f32[200,128]{1,0:T(8,128)S(1)} %get-tuple-element.36), channel_id=1, source_target_pairs={{0,32},{8,40},{16,48},{24,56},{32,0},{40,8},{48,16},{56,24},{64,96... | collective-permute-start | bytes 307208 | tf_op jit(solution)/shard_map/ppermute | solution.py:489
  29.1 0.0 collective-permute-done.refs_9_
  29.1 0.0 collective-permute-done.1.refs_10_
  29.1 10.7 %first_interior.1 = (f32[7,48,16,128]{3,2,1,0:T(8,128)S(1)}, f32[7,48,16,128]{3,2,1,0:T(8,128)}, f32[112,128]{1,0:T(8,128)S(1)}, f32[112,128]{1,0:T(8,128)S(1)},...) custom-call(s32[2]{0:T(128)S(1)} %pad_add_fusion.info.refs_0_, ...), custom_call_target="tpu_custom_call" | custom-call | flops 30000000 | bytes 12000000 | tf_op jit(solution)/shard_map/first_interior/pallas_call | solution.py:377
  39.8 1.5 %copy-done.1 = f32[7,48,16,128]{3,2,1,0:T(8,128)} copy-done((f32[7,48,16,128]{3,2,1,0:T(8,128)}, f32[7,48,16,128]{3,2,1,0:T(8,128)S(1)}, u32[]{:S(2)}) %copy-start.1) | copy-done | bytes 2752536
  41.3 0.0 collective-permute-done.9.refs_1_
  41.3 0.0 collective-permute-done.10.refs_2_
  41.3 0.8 boundary.1
  42.1 2.8 %collective-permute-start.16 = (f32[200,128]{1,0:T(8,128)S(1)}, f32[200,128]{1,0:T(8,128)S(1)}, u32[]{:S(2)}, u32[]{:S(2)}) collective-permute-start(f32[200,128]{1,0:T(8,128)S(1)} %get-tuple-element.46.refs_0_), channel_id=1, source_target_pairs={{0,192},{8,200},{16,208},{24,216},{32,224},{40,232},{48,240},{56,2... | collective-permute-start | bytes 307208 | tf_op jit(solution)/shard_map/ppermute | solution.py:489
  44.9 0.8 %collective-permute-start.15 = (f32[200,128]{1,0:T(8,128)S(1)}, f32[200,128]{1,0:T(8,128)S(1)}, u32[]{:S(2)}, u32[]{:S(2)}) collective-permute-start(f32[200,128]{1,0:T(8,128)S(1)} %get-tuple-element.46.refs_0_), channel_id=1, source_target_pairs={{0,128},{8,136},{16,144},{24,152},{32,160},{40,168},{48,176},{56,1... | collective-permute-start | bytes 307208 | tf_op jit(solution)/shard_map/ppermute | solution.py:489
  45.7 0.5 collective-permute-start.14
  46.3 0.0 collective-permute-start.17
  46.3 2.8 %collective-permute-done.16.refs_3_ = f32[200,128]{1,0:T(8,128)S(1)} collective-permute-done((f32[200,128]{1,0:T(8,128)S(1)}, f32[200,128]{1,0:T(8,128)S(1)}, u32[]{:S(2)}, u32[]{:S(2)}) %collective-permute-start.16) | collective-permute-done | bytes 102432 | tf_op jit(solution)/shard_map/ppermute | solution.py:489
  49.1 2.6 %collective-permute-done.15.refs_2_ = f32[200,128]{1,0:T(8,128)S(1)} collective-permute-done((f32[200,128]{1,0:T(8,128)S(1)}, f32[200,128]{1,0:T(8,128)S(1)}, u32[]{:S(2)}, u32[]{:S(2)}) %collective-permute-start.15) | collective-permute-done | bytes 102432 | tf_op jit(solution)/shard_map/ppermute | solution.py:489
  51.6 0.0 collective-permute-start.19
  51.6 0.5 collective-permute-start.18
  52.1 1.9 %collective-permute-start.12 = (f32[7,48,128]{2,1,0:T(8,128)S(1)}, f32[7,48,128]{2,1,0:T(8,128)S(1)}, u32[]{:S(2)}, u32[]{:S(2)}) collective-permute-start(f32[7,48,128]{2,1,0:T(8,128)S(1)} %get-tuple-element.44), channel_id=1, source_target_pairs={{0,1},{1,2},{2,3},{3,4},{4,5},{5,6},{6,7},{8,9},{9,10},{10,11},{11... | collective-permute-start | bytes 516104 | tf_op jit(solution)/shard_map/ppermute | solution.py:496
  54.1 0.0 collective-permute-done.17.refs_4_
  54.1 6.0 %collective-permute-start.13 = (f32[7,48,128]{2,1,0:T(8,128)S(1)}, f32[7,48,128]{2,1,0:T(8,128)S(1)}, u32[]{:S(2)}, u32[]{:S(2)}) collective-permute-start(f32[7,48,128]{2,1,0:T(8,128)S(1)} %get-tuple-element.45), channel_id=1, source_target_pairs={{1,0},{2,1},{3,2},{4,3},{5,4},{6,5},{7,6},{9,8},{10,9},{11,10},{12... | collective-permute-start | bytes 516104 | tf_op jit(solution)/shard_map/ppermute | solution.py:496
  60.1 0.0 collective-permute-done.20.refs_7_
  60.1 0.0 collective-permute-done.19.refs_6_
  60.1 1.9 %relay.3 = (f32[200,128]{1,0:T(8,128)S(1)}, f32[200,128]{1,0:T(8,128)S(1)}, f32[200,128]{1,0:T(8,128)S(1)}, f32[200,128]{1,0:T(8,128)S(1)}) custom-call(s32[2]{0:T(128)S(1)} %pad_add_fusion.info.refs_0_, s32[32]{0:T(128)S(1)} %copy-done.7, s32[32,4,128]{2,1,0:T(4,128)S(1)} %copy.17.ids_ref, f32[32,4,128]{2,1,0:T(4,128)S(1)} %copy.18.shares_ref, ...), custom_call_target="tpu_custom_call" | custom-call | tf_op jit(solution)/shard_map/relay/pallas_call | solution.py:215
  62.0 1.8 %collective-permute-start.21 = (f32[200,128]{1,0:T(8,128)S(1)}, f32[200,128]{1,0:T(8,128)S(1)}, u32[]{:S(2)}, u32[]{:S(2)}) collective-permute-start(f32[200,128]{1,0:T(8,128)S(1)} %get-tuple-element.50), channel_id=1, source_target_pairs={{0,16},{8,24},{16,0},{24,8},{32,48},{40,56},{48,32},{56,40},{64,80... | collective-permute-start | bytes 307208 | tf_op jit(solution)/shard_map/ppermute | solution.py:489
  63.8 4.5 %collective-permute-start.22 = (f32[200,128]{1,0:T(8,128)S(1)}, f32[200,128]{1,0:T(8,128)S(1)}, u32[]{:S(2)}, u32[]{:S(2)}) collective-permute-start(f32[200,128]{1,0:T(8,128)S(1)} %get-tuple-element.51), channel_id=1, source_target_pairs={{0,32},{8,40},{16,48},{24,56},{32,0},{40,8},{48,16},{56,24},{64,96... | collective-permute-start | bytes 307208 | tf_op jit(solution)/shard_map/ppermute | solution.py:489
  68.3 0.3 collective-permute-start.23
  68.6 8.0 %second_interior.1 = f32[7,48,16,128]{3,2,1,0:T(8,128)S(1)} custom-call(s32[2]{0:T(128)S(1)} %pad_add_fusion.info.refs_0_, f32[7,7]{1,0:T(8,128)S(1)} %copy-done.6, f32[7,768,128]{2,1,0:T(8,128)} %bitcast.21, f32[7,48,16,128]{3,2,1,0:T(8,128)} %get-tuple-element.34.refs_3_, f32[48,16,128]{2,1,0:T(8,128)S(1)} %bitcast.23, f32[48,16,128]{2,1,0:T(8,128)S(1)} %bitcast.25, ...), custom_call_target="tpu_custom_call" | custom-call | flops 30000000 | bytes 12000000 | tf_op jit(solution)/shard_map/second_interior/pallas_call | solution.py:377
  76.7 3.4 %correct_final.1 = f32[7,768,128]{2,1,0:T(8,128)} custom-call(s32[2]{0:T(128)S(1)} %pad_add_fusion.info.refs_0_, f32[7,768,128]{2,1,0:T(8,128)S(1)} %bitcast.18, f32[200,128]{1,0:T(8,128)S(1)} %get-tuple-element.47.refs_10_.refs_0_, f32[200,128]{1,0:T(8,128)S(1)} %collective-permute-done.21.refs_1_, f32[200,128]{1,0:T(8,128)S(1)} %collective-permute-done.22.refs_2_, ...), custom_call_target="tpu_custom_call" | custom-call | tf_op jit(solution)/shard_map/correct_final/pallas_call | solution.py:475
  (35 shorter events, 0.1 us)
Async XLA Ops:
  0.0 18.2 %copy-start.9 = (s32[32,8,4]{0,2,1:T(4,128)S(1)}, s32[32,8,4]{0,2,1:T(4,128)}, u32[]{:S(2)}) copy-start(s32[32,8,4]{0,2,1:T(4,128)} %param.21) | copy-start | bytes 12292
  0.0 18.2 %copy-start.8 = (s32[32,8,4]{0,2,1:T(4,128)S(1)}, s32[32,8,4]{0,2,1:T(4,128)}, u32[]{:S(2)}) copy-start(s32[32,8,4]{0,2,1:T(4,128)} %param.20) | copy-start | bytes 12292
  0.0 19.3 %copy-start.7 = (s32[32]{0:T(128)S(1)}, s32[32]{0:T(128)}, u32[]{:S(2)}) copy-start(s32[32]{0:T(128)} %partner.3) | copy-start | bytes 388
  0.0 29.1 %copy-start.6 = (f32[7,7]{1,0:T(8,128)S(1)}, f32[7,7]{1,0:T(8,128)}, u32[]{:S(2)}) copy-start(f32[7,7]{1,0:T(8,128)} %refs_1_.3) | copy-start | bytes 592
  0.1 1.8 %copy-start = (f32[7,1,48,16,128]{4,3,2,1,0:T(8,128)S(1)}, f32[7,1,48,16,128]{4,3,2,1,0:T(8,128)}, u32[]{:S(2)}) copy-start(f32[7,1,48,16,128]{4,3,2,1,0:T(8,128)} %param.11) | copy-start | bytes 8257540
  1.9 27.2 %copy-start.2 = (f32[1,48,16,128]{3,2,1,0:T(8,128)S(1)}, f32[1,48,16,128]{3,2,1,0:T(8,128)}, u32[]{:S(2)}) copy-start(f32[1,48,16,128]{3,2,1,0:T(8,128)} %param.14) | copy-start | bytes 1179652
  1.9 27.2 %copy-start.3 = (f32[1,48,16,128]{3,2,1,0:T(8,128)S(1)}, f32[1,48,16,128]{3,2,1,0:T(8,128)}, u32[]{:S(2)}) copy-start(f32[1,48,16,128]{3,2,1,0:T(8,128)} %param.15) | copy-start | bytes 1179652
  1.9 27.2 %copy-start.4 = (f32[1,48,16,128]{3,2,1,0:T(8,128)S(1)}, f32[1,48,16,128]{3,2,1,0:T(8,128)}, u32[]{:S(2)}) copy-start(f32[1,48,16,128]{3,2,1,0:T(8,128)} %param.16) | copy-start | bytes 1179652
  1.9 27.2 %copy-start.5 = (f32[7,16,128]{2,1,0:T(8,128)S(1)}, f32[7,16,128]{2,1,0:T(8,128)}, u32[]{:S(2)}) copy-start(f32[7,16,128]{2,1,0:T(8,128)} %refs_7_.1) | copy-start | bytes 172036
  5.2 7.8 %collective-permute-start.5 = (f32[200,128]{1,0:T(8,128)S(1)}, f32[200,128]{1,0:T(8,128)S(1)}, u32[]{:S(2)}, u32[]{:S(2)}) collective-permute-start(f32[200,128]{1,0:T(8,128)S(1)} %get-tuple-element.31.refs_0_), channel_id=1, source_target_pairs={{0,8},{8,0},{16,24},{24,16},{32,40},{40,32},{48,56},{56,48},{64,72... | collective-permute-start | bytes 307208 | tf_op jit(solution)/shard_map/ppermute | solution.py:489
  5.3 12.2 %collective-permute-start.4 = (f32[200,128]{1,0:T(8,128)S(1)}, f32[200,128]{1,0:T(8,128)S(1)}, u32[]{:S(2)}, u32[]{:S(2)}) collective-permute-start(f32[200,128]{1,0:T(8,128)S(1)} %get-tuple-element.31.refs_0_), channel_id=1, source_target_pairs={{0,192},{8,200},{16,208},{24,216},{32,224},{40,232},{48,240},{56,2... | collective-permute-start | bytes 307208 | tf_op jit(solution)/shard_map/ppermute | solution.py:489
  8.1 9.4 %collective-permute-start.3 = (f32[200,128]{1,0:T(8,128)S(1)}, f32[200,128]{1,0:T(8,128)S(1)}, u32[]{:S(2)}, u32[]{:S(2)}) collective-permute-start(f32[200,128]{1,0:T(8,128)S(1)} %get-tuple-element.31.refs_0_), channel_id=1, source_target_pairs={{0,128},{8,136},{16,144},{24,152},{32,160},{40,168},{48,176},{56,1... | collective-permute-start | bytes 307208 | tf_op jit(solution)/shard_map/ppermute | solution.py:489
  8.9 9.1 %collective-permute-start.2 = (f32[200,128]{1,0:T(8,128)S(1)}, f32[200,128]{1,0:T(8,128)S(1)}, u32[]{:S(2)}, u32[]{:S(2)}) collective-permute-start(f32[200,128]{1,0:T(8,128)S(1)} %get-tuple-element.31.refs_0_), channel_id=1, source_target_pairs={{0,64},{8,72},{16,80},{24,88},{32,96},{40,104},{48,112},{56,120},{... | collective-permute-start | bytes 307208 | tf_op jit(solution)/shard_map/ppermute | solution.py:489
  9.5 19.6 %collective-permute-start = (f32[7,48,128]{2,1,0:T(8,128)S(1)}, f32[7,48,128]{2,1,0:T(8,128)S(1)}, u32[]{:S(2)}, u32[]{:S(2)}) collective-permute-start(f32[7,48,128]{2,1,0:T(8,128)S(1)} %get-tuple-element.29), channel_id=1, source_target_pairs={{0,1},{1,2},{2,3},{3,4},{4,5},{5,6},{6,7},{8,9},{9,10},{10,11},{11... | collective-permute-start | bytes 516104 | tf_op jit(solution)/shard_map/ppermute | solution.py:496
  13.0 16.1 %collective-permute-start.1 = (f32[7,48,128]{2,1,0:T(8,128)S(1)}, f32[7,48,128]{2,1,0:T(8,128)S(1)}, u32[]{:S(2)}, u32[]{:S(2)}) collective-permute-start(f32[7,48,128]{2,1,0:T(8,128)S(1)} %get-tuple-element.30), channel_id=1, source_target_pairs={{1,0},{2,1},{3,2},{4,3},{5,4},{6,5},{7,6},{9,8},{10,9},{11,10},{12... | collective-permute-start | bytes 516104 | tf_op jit(solution)/shard_map/ppermute | solution.py:496
  17.4 1.4 %collective-permute-start.8 = (f32[200,128]{1,0:T(8,128)S(1)}, f32[200,128]{1,0:T(8,128)S(1)}, u32[]{:S(2)}, u32[]{:S(2)}) collective-permute-start(f32[200,128]{1,0:T(8,128)S(1)} %collective-permute-done.4.refs_3_), channel_id=1, source_target_pairs={{0,8},{8,0},{16,24},{24,16},{32,40},{40,32},{48,56},{56,48},{64,72... | collective-permute-start | bytes 307208 | tf_op jit(solution)/shard_map/ppermute | solution.py:489
  17.5 1.4 %collective-permute-start.7 = (f32[200,128]{1,0:T(8,128)S(1)}, f32[200,128]{1,0:T(8,128)S(1)}, u32[]{:S(2)}, u32[]{:S(2)}) collective-permute-start(f32[200,128]{1,0:T(8,128)S(1)} %collective-permute-done.3.refs_2_), channel_id=1, source_target_pairs={{0,8},{8,0},{16,24},{24,16},{32,40},{40,32},{48,56},{56,48},{64,72... | collective-permute-start | bytes 307208 | tf_op jit(solution)/shard_map/ppermute | solution.py:489
  18.0 1.3 %collective-permute-start.6 = (f32[200,128]{1,0:T(8,128)S(1)}, f32[200,128]{1,0:T(8,128)S(1)}, u32[]{:S(2)}, u32[]{:S(2)}) collective-permute-start(f32[200,128]{1,0:T(8,128)S(1)} %collective-permute-done.2.refs_1_), channel_id=1, source_target_pairs={{0,8},{8,0},{16,24},{24,16},{32,40},{40,32},{48,56},{56,48},{64,72... | collective-permute-start | bytes 307208 | tf_op jit(solution)/shard_map/ppermute | solution.py:489
  21.2 20.1 %collective-permute-start.9 = (f32[200,128]{1,0:T(8,128)S(1)}, f32[200,128]{1,0:T(8,128)S(1)}, u32[]{:S(2)}, u32[]{:S(2)}) collective-permute-start(f32[200,128]{1,0:T(8,128)S(1)} %get-tuple-element.35), channel_id=1, source_target_pairs={{0,16},{8,24},{16,0},{24,8},{32,48},{40,56},{48,32},{56,40},{64,80... | collective-permute-start | bytes 307208 | tf_op jit(solution)/shard_map/ppermute | solution.py:489
  24.6 16.7 %collective-permute-start.10 = (f32[200,128]{1,0:T(8,128)S(1)}, f32[200,128]{1,0:T(8,128)S(1)}, u32[]{:S(2)}, u32[]{:S(2)}) collective-permute-start(f32[200,128]{1,0:T(8,128)S(1)} %get-tuple-element.36), channel_id=1, source_target_pairs={{0,32},{8,40},{16,48},{24,56},{32,0},{40,8},{48,16},{56,24},{64,96... | collective-permute-start | bytes 307208 | tf_op jit(solution)/shard_map/ppermute | solution.py:489
  29.0 12.2 %collective-permute-start.11 = (f32[200,128]{1,0:T(8,128)S(1)}, f32[200,128]{1,0:T(8,128)S(1)}, u32[]{:S(2)}, u32[]{:S(2)}) collective-permute-start(f32[200,128]{1,0:T(8,128)S(1)} %get-tuple-element.37), channel_id=1, source_target_pairs={{0,48},{8,56},{16,32},{24,40},{32,16},{40,24},{48,0},{56,8},{64,11... | collective-permute-start | bytes 307208 | tf_op jit(solution)/shard_map/ppermute | solution.py:489
  39.8 1.5 %copy-start.1 = (f32[7,48,16,128]{3,2,1,0:T(8,128)}, f32[7,48,16,128]{3,2,1,0:T(8,128)S(1)}, u32[]{:S(2)}) copy-start(f32[7,48,16,128]{3,2,1,0:T(8,128)S(1)} %get-tuple-element.33) | copy-start | bytes 8257540
  42.1 7.0 %collective-permute-start.16 = (f32[200,128]{1,0:T(8,128)S(1)}, f32[200,128]{1,0:T(8,128)S(1)}, u32[]{:S(2)}, u32[]{:S(2)}) collective-permute-start(f32[200,128]{1,0:T(8,128)S(1)} %get-tuple-element.46.refs_0_), channel_id=1, source_target_pairs={{0,192},{8,200},{16,208},{24,216},{32,224},{40,232},{48,240},{56,2... | collective-permute-start | bytes 307208 | tf_op jit(solution)/shard_map/ppermute | solution.py:489
  44.9 6.7 %collective-permute-start.15 = (f32[200,128]{1,0:T(8,128)S(1)}, f32[200,128]{1,0:T(8,128)S(1)}, u32[]{:S(2)}, u32[]{:S(2)}) collective-permute-start(f32[200,128]{1,0:T(8,128)S(1)} %get-tuple-element.46.refs_0_), channel_id=1, source_target_pairs={{0,128},{8,136},{16,144},{24,152},{32,160},{40,168},{48,176},{56,1... | collective-permute-start | bytes 307208 | tf_op jit(solution)/shard_map/ppermute | solution.py:489
  45.7 5.9 %collective-permute-start.14 = (f32[200,128]{1,0:T(8,128)S(1)}, f32[200,128]{1,0:T(8,128)S(1)}, u32[]{:S(2)}, u32[]{:S(2)}) collective-permute-start(f32[200,128]{1,0:T(8,128)S(1)} %get-tuple-element.46.refs_0_), channel_id=1, source_target_pairs={{0,64},{8,72},{16,80},{24,88},{32,96},{40,104},{48,112},{56,120},{... | collective-permute-start | bytes 307208 | tf_op jit(solution)/shard_map/ppermute | solution.py:489
  46.3 7.8 %collective-permute-start.17 = (f32[200,128]{1,0:T(8,128)S(1)}, f32[200,128]{1,0:T(8,128)S(1)}, u32[]{:S(2)}, u32[]{:S(2)}) collective-permute-start(f32[200,128]{1,0:T(8,128)S(1)} %get-tuple-element.46.refs_0_), channel_id=1, source_target_pairs={{0,8},{8,0},{16,24},{24,16},{32,40},{40,32},{48,56},{56,48},{64,72... | collective-permute-start | bytes 307208 | tf_op jit(solution)/shard_map/ppermute | solution.py:489
  49.1 11.1 %collective-permute-start.20 = (f32[200,128]{1,0:T(8,128)S(1)}, f32[200,128]{1,0:T(8,128)S(1)}, u32[]{:S(2)}, u32[]{:S(2)}) collective-permute-start(f32[200,128]{1,0:T(8,128)S(1)} %collective-permute-done.16.refs_3_), channel_id=1, source_target_pairs={{0,8},{8,0},{16,24},{24,16},{32,40},{40,32},{48,56},{56,48},{64,72... | collective-permute-start | bytes 307208 | tf_op jit(solution)/shard_map/ppermute | solution.py:489
  51.6 8.5 %collective-permute-start.19 = (f32[200,128]{1,0:T(8,128)S(1)}, f32[200,128]{1,0:T(8,128)S(1)}, u32[]{:S(2)}, u32[]{:S(2)}) collective-permute-start(f32[200,128]{1,0:T(8,128)S(1)} %collective-permute-done.15.refs_2_), channel_id=1, source_target_pairs={{0,8},{8,0},{16,24},{24,16},{32,40},{40,32},{48,56},{56,48},{64,72... | collective-permute-start | bytes 307208 | tf_op jit(solution)/shard_map/ppermute | solution.py:489
  51.6 8.5 %collective-permute-start.18 = (f32[200,128]{1,0:T(8,128)S(1)}, f32[200,128]{1,0:T(8,128)S(1)}, u32[]{:S(2)}, u32[]{:S(2)}) collective-permute-start(f32[200,128]{1,0:T(8,128)S(1)} %collective-permute-done.14.refs_1_), channel_id=1, source_target_pairs={{0,8},{8,0},{16,24},{24,16},{32,40},{40,32},{48,56},{56,48},{64,72... | collective-permute-start | bytes 307208 | tf_op jit(solution)/shard_map/ppermute | solution.py:489
  52.1 16.4 %collective-permute-start.12 = (f32[7,48,128]{2,1,0:T(8,128)S(1)}, f32[7,48,128]{2,1,0:T(8,128)S(1)}, u32[]{:S(2)}, u32[]{:S(2)}) collective-permute-start(f32[7,48,128]{2,1,0:T(8,128)S(1)} %get-tuple-element.44), channel_id=1, source_target_pairs={{0,1},{1,2},{2,3},{3,4},{4,5},{5,6},{6,7},{8,9},{9,10},{10,11},{11... | collective-permute-start | bytes 516104 | tf_op jit(solution)/shard_map/ppermute | solution.py:496
  54.1 14.5 %collective-permute-start.13 = (f32[7,48,128]{2,1,0:T(8,128)S(1)}, f32[7,48,128]{2,1,0:T(8,128)S(1)}, u32[]{:S(2)}, u32[]{:S(2)}) collective-permute-start(f32[7,48,128]{2,1,0:T(8,128)S(1)} %get-tuple-element.45), channel_id=1, source_target_pairs={{1,0},{2,1},{3,2},{4,3},{5,4},{6,5},{7,6},{9,8},{10,9},{11,10},{12... | collective-permute-start | bytes 516104 | tf_op jit(solution)/shard_map/ppermute | solution.py:496
  62.0 14.7 %collective-permute-start.21 = (f32[200,128]{1,0:T(8,128)S(1)}, f32[200,128]{1,0:T(8,128)S(1)}, u32[]{:S(2)}, u32[]{:S(2)}) collective-permute-start(f32[200,128]{1,0:T(8,128)S(1)} %get-tuple-element.50), channel_id=1, source_target_pairs={{0,16},{8,24},{16,0},{24,8},{32,48},{40,56},{48,32},{56,40},{64,80... | collective-permute-start | bytes 307208 | tf_op jit(solution)/shard_map/ppermute | solution.py:489
  63.8 12.9 %collective-permute-start.22 = (f32[200,128]{1,0:T(8,128)S(1)}, f32[200,128]{1,0:T(8,128)S(1)}, u32[]{:S(2)}, u32[]{:S(2)}) collective-permute-start(f32[200,128]{1,0:T(8,128)S(1)} %get-tuple-element.51), channel_id=1, source_target_pairs={{0,32},{8,40},{16,48},{24,56},{32,0},{40,8},{48,16},{56,24},{64,96... | collective-permute-start | bytes 307208 | tf_op jit(solution)/shard_map/ppermute | solution.py:489
  68.3 8.4 %collective-permute-start.23 = (f32[200,128]{1,0:T(8,128)S(1)}, f32[200,128]{1,0:T(8,128)S(1)}, u32[]{:S(2)}, u32[]{:S(2)}) collective-permute-start(f32[200,128]{1,0:T(8,128)S(1)} %get-tuple-element.52), channel_id=1, source_target_pairs={{0,48},{8,56},{16,32},{24,40},{32,16},{40,24},{48,0},{56,8},{64,11... | collective-permute-start | bytes 307208 | tf_op jit(solution)/shard_map/ppermute | solution.py:489

commit v3 on v2

--- a/solution.py
+++ b/solution.py
@@ -87,7 +87,7 @@
     )
 
 
-def add_terms(info, ref, base, c, edge_add, face_add):
+def add_terms(info, old, ref, base, c, edge_add, face_add):
     fields, width = ref.shape[0], ref.shape[2]
     side = info[1] * (DEPTH - 1)
     lane = lanes()
@@ -101,7 +101,7 @@
             for j in range(LAYERS):
                 rows = pl.ds(pl.multiple_of(start + 16 * j + 8 * h, 8), 8)
                 here = pltpu.roll(turned, width - 1 - 2 * (LAYERS - 1 - j), 1)
-                ref[f, rows, :] = ref[f, rows, :] + jnp.where(ends, here, 0.0)
+                ref[f, rows, :] = old[f, rows, :] + jnp.where(ends, here, 0.0)
         return 0
 
     lax.fori_loop(0, fields, one, 0, unroll=True)
@@ -113,17 +113,13 @@
             ref[f, rows, :] = ref[f, rows, :] + face_add[16 * f : 16 * f + 16, :]
 
 
-def pack_kernel(info, s_hbm, packet, low, high, units, s_ref, sem):
+def pack_kernel(info, s_ref, packet, low, high, units):
     fields, rows, width = s_ref.shape
-    copies = [pltpu.make_async_copy(s_hbm.at[f], s_ref.at[f], sem.at[f]) for f in range(fields)]
-    for copy in copies:
-        copy.start()
     depth = rows // 16
     pair = lanes() >> 1
     start = info[1] * (rows - 16)
 
     def one(f, _):
-        pltpu.make_async_copy(s_hbm.at[f], s_ref.at[f], sem.at[f]).wait()
         row = pl.multiple_of(f * 16, 16)
         packet[pl.ds(row, 16), :] = s_ref[f, pl.ds(pl.multiple_of(start, 16), 16), :]
         for h in range(2):
@@ -148,13 +144,9 @@
     return pl.pallas_call(
         pack_kernel,
         out_shape=(struct(EDGE + 8 * TIGHT, width), row, row),
-        in_specs=[SMEM, ANY],
+        in_specs=[SMEM, VMEM],
         out_specs=(VMEM, VMEM, VMEM),
-        scratch_shapes=[
-            pltpu.VMEM((EDGE, width), jnp.float32),
-            pltpu.VMEM(cells.shape, jnp.float32),
-            pltpu.SemaphoreType.DMA((fields,)),
-        ],
+        scratch_shapes=[pltpu.VMEM((EDGE, width), jnp.float32)],
         compiler_params=params(48),
         name="pack",
     )(info, cells)
@@ -229,11 +221,11 @@
 def interior_kernel(first, *refs):
     if first:
         info, coupling, v_hbm, prior, older, axial, pitch, visc, inflow, halo_low, halo_high, _ = refs[:12]
-        (out, base, face, edges, edge_coef, face_coef, low, high) = refs[12:20]
-        line, sem, ends = refs[20:]
+        (out, face, edges, edge_coef, face_coef, low, high) = refs[12:19]
+        line, sem, ends = refs[19:]
     else:
-        (info, coupling, v_hbm, base, axial, pitch, visc, inflow, halo_low, halo_high, _) = refs[:11]
-        edge_add, face_add, out, line, sem = refs[11:]
+        info, coupling, v_hbm, prior, older, axial, pitch, visc, inflow, halo_low, halo_high, _ = refs[:12]
+        edge_add, face_add, out, line, sem = refs[12:]
     fields, rows, width = line.shape[0], line.shape[1] - 32, line.shape[2]
     depth = rows // 16
     step = pl.program_id(0)
@@ -245,7 +237,7 @@
     def ready(c):
         chunk_copy(v_hbm, line, sem, c, 16).wait()
         if not first:
-            add_terms(info, line, 16, c, edge_add, face_add)
+            add_terms(info, line, line, 16, c, edge_add, face_add)
 
         @pl.when(c == chunks - 1)
         def _():
@@ -317,17 +309,16 @@
                     - dt * mixed
                 )
                 place = (f, j, slice(8 * h, 8 * h + 8))
+                change = change + dt * (prior[place] - 0.25 * older[place])
                 if first:
-                    known = dt * (prior[place] - 0.25 * older[place])
-                    base[place] = known
-                    moved = x + 0.5 * (known + change)
+                    moved = x + 0.5 * change
                     out[place] = moved
                     if h == 0:
                         low[f, pl.ds(j, 1), :] = moved[0:1]
                     else:
                         high[f, pl.ds(j, 1), :] = moved[7:8]
                 else:
-                    out[place] = x + (base[place] + change)
+                    out[place] = x + change
         return 0
 
     lax.fori_loop(0, LAYERS, one, 0, unroll=4)
@@ -370,8 +361,8 @@
     out_shape, out_specs = [whole], [block]
     if first:
         small = [(EDGE, width), (EDGE, width), (16, width), (16, width)]
-        out_shape += [whole] + [struct(*s) for s in small]
-        out_specs += [block] + [fixed(*s) for s in small]
+        out_shape += [struct(*s) for s in small]
+        out_specs += [fixed(*s) for s in small]
         out_shape += [struct(fields, depth, width)] * 2
         out_specs += [pl.BlockSpec((fields, LAYERS, width), lambda i: (0, i, 0))] * 2
     return pl.pallas_call(
@@ -389,7 +380,7 @@
             pltpu.SemaphoreType.DMA((depth // LAYERS,)),
         ]
         + [pltpu.VMEM((LAYERS, 16, width), jnp.float32)] * int(first),
-        compiler_params=params(48),
+        compiler_params=params(48 if first else 42),
         cost_estimate=pl.CostEstimate(flops=30_000_000, bytes_accessed=12_000_000, transcendentals=0),
         name="first_interior" if first else "second_interior",
     )(info, coupling, v, *given, *speeds, inflow, *halos, order, *adds)
@@ -450,18 +441,15 @@
 
 
 def final_kernel(info, v, *refs):
-    parts, (edge_coef, face_coef, out, held, edge_add, face_add, arrived, left) = refs[:4], refs[4:]
+    parts, (edge_coef, face_coef, out, held, edge_add, face_add, left) = refs[:4], refs[4:]
     chunks = DEPTH // LAYERS
-    for c in range(chunks):
-        chunk_copy(v, held, arrived, c).start()
     edge_terms, face_terms = terms(1.0, parts, edge_coef, face_coef)
     for u in range(UNITS):
         edge_add[8 * u : 8 * u + 8, :] = edge_terms[u]
         face_add[8 * u : 8 * u + 8, :] = face_terms[u]
 
     def one(c, _):
-        chunk_copy(v, held, arrived, c).wait()
-        add_terms(info, held, 0, c, edge_add, face_add)
+        add_terms(info, v, held, 0, c, edge_add, face_add)
         chunk_copy(held, out, left, c).start()
         return 0
 
@@ -475,11 +463,11 @@
     return pl.pallas_call(
         final_kernel,
         out_shape=struct(*v.shape),
-        in_specs=[SMEM, ANY] + [VMEM] * 6,
+        in_specs=[SMEM] + [VMEM] * 7,
         out_specs=ANY,
         scratch_shapes=[pltpu.VMEM(v.shape, jnp.float32)]
         + [pltpu.VMEM((EDGE, width), jnp.float32)] * 2
-        + [pltpu.SemaphoreType.DMA((DEPTH // LAYERS,))] * 2,
+        + [pltpu.SemaphoreType.DMA((DEPTH // LAYERS,))],
         compiler_params=params(48),
         name="correct_final",
     )(info, v, *parts, edge_coef, face_coef)
@@ -516,6 +504,7 @@
     fields, _, depth, spans, width = state.shape
     cells = state.reshape(fields, depth * spans, width)
     speeds = (axial_speed[0], pitch_speed[0], viscosity[0])
+    levels = (previous[:, 0], earlier[:, 0])
     weights = tile_weights.astype(jnp.float32)
     shares = weights / jnp.sum(weights, axis=2, keepdims=True)
     cut = width // tile_ids.shape[1]
@@ -531,8 +520,8 @@
     packet, low, high = pack(info, cells)
     parts = exchange(packet)
     halos = span_halos(low, high)
-    middle, base, face, edges, edge_coef, face_coef, low, high = interior(
-        True, info, coupling, cells, (previous[:, 0], earlier[:, 0]), speeds, inflow, halos, parts[0]
+    middle, face, edges, edge_coef, face_coef, low, high = interior(
+        True, info, coupling, cells, levels, speeds, inflow, halos, parts[0]
     )
     packet, edge_add, face_add, low, high = boundary(
         info, parts, face, edges, edge_coef, face_coef, low, high
@@ -544,7 +533,7 @@
         info,
         coupling,
         middle.reshape(cells.shape),
-        (base,),
+        levels,
         speeds,
         inflow,
         halos,

time: 80.7 us -> 76.2 us (0.944)
  Pallas kernels: 29.8 us -> 27 us
  local copies, waits for them, and re-layouts: 3.57 us -> 2.08 us
    unnamed x20, local copies, waits for them, and re-layouts: 3.31 us -> 1.81 us
    pallas_call x1, Pallas kernels: 3.27 us -> 1.89 us  [pack(): pl.pallas_call(pack_kernel, out_shape=(struct(EDGE + 8 * TIGHT, width), r...]
    pallas_call x2, Pallas kernels: 18.7 us -> 17.6 us  [interior(): pl.pallas_call(functools.partial(interior_kernel, first), grid=(depth //...]
where the time goes in v3:
time: 76.2 us; the launch traced here: 75.8 us
  starting transfers between devices  39.9 us (52%)
  Pallas kernels  27 us (35%)
  waiting for transfers between devices  6.25 us (8%)
  local copies, waits for them, and re-layouts  2.08 us (3%)
    ppermute x20, starting transfers between devices, flip(): lax.ppermute(value, 'passage', [(i, i ^ bits) for i in range(lax.axis_siz...  24.1 us
    pallas_call x2, Pallas kernels, interior(): pl.pallas_call(functools.partial(interior_kernel, first), grid=(depth //...  17.6 us
    ppermute x4, starting transfers between devices, span_halos(): return (lax.ppermute(high, 'span', up), lax.ppermute(low, 'span', down))  15.9 us
    ppermute x20, waiting for transfers between devices, flip(): lax.ppermute(value, 'passage', [(i, i ^ bits) for i in range(lax.axis_siz...  6.24 us
    pallas_call x2, Pallas kernels, relay(): pl.pallas_call(relay_kernel, out_shape=(struct(*packets[0].shape),) * 4,...  3.69 us
    pallas_call x1, Pallas kernels, correct_final(): pl.pallas_call(final_kernel, out_shape=struct(*v.shape), in_specs=[SMEM]...  3.02 us
    pallas_call x1, Pallas kernels, pack(): pl.pallas_call(pack_kernel, out_shape=(struct(EDGE + 8 * TIGHT, width), r...  1.89 us
    unnamed x20, local copies, waits for them, and re-layouts  1.81 us
  transfers between devices with their start and end apart: 24, of which 5 were waited for; matrix products, arithmetic and copies ran while one was open for 0% of the time, Pallas kernels for 28%

profile of v3, /device:TPU:32, one launch (start us, length us, event | category | flops | bytes accessed | tf_op | source)
XLA Modules:
  0.0 75.8 jit_solution(17801106971836404400)
XLA Ops:
  0.0 0.1 pad_add_fusion.info.refs_0_
  0.1 1.8 %copy-done = f32[7,1,48,16,128]{4,3,2,1,0:T(8,128)S(1)} copy-done((f32[7,1,48,16,128]{4,3,2,1,0:T(8,128)S(1)}, f32[7,1,48,16,128]{4,3,2,1,0:T(8,128)}, u32[]{:S(2)}) %copy-start) | copy-done | bytes 2752536
  1.9 1.9 %pack.1 = (f32[200,128]{1,0:T(8,128)S(1)}, f32[7,48,128]{2,1,0:T(8,128)S(1)}, f32[7,48,128]{2,1,0:T(8,128)S(1)}) custom-call(s32[2]{0:T(128)S(1)} %pad_add_fusion.info.refs_0_, f32[7,768,128]{2,1,0:T(8,128)S(1)} %bitcast.19), custom_call_target="tpu_custom_call" | custom-call | tf_op jit(solution)/shard_map/pack/pallas_call | solution.py:144
  3.8 0.1 collective-permute-start.5
  3.9 2.8 %collective-permute-start.4 = (f32[200,128]{1,0:T(8,128)S(1)}, f32[200,128]{1,0:T(8,128)S(1)}, u32[]{:S(2)}, u32[]{:S(2)}) collective-permute-start(f32[200,128]{1,0:T(8,128)S(1)} %get-tuple-element.30.refs_0_), channel_id=1, source_target_pairs={{0,192},{8,200},{16,208},{24,216},{32,224},{40,232},{48,240},{56,2... | collective-permute-start | bytes 307208 | tf_op jit(solution)/shard_map/ppermute | solution.py:477
  6.7 0.8 %collective-permute-start.3 = (f32[200,128]{1,0:T(8,128)S(1)}, f32[200,128]{1,0:T(8,128)S(1)}, u32[]{:S(2)}, u32[]{:S(2)}) collective-permute-start(f32[200,128]{1,0:T(8,128)S(1)} %get-tuple-element.30.refs_0_), channel_id=1, source_target_pairs={{0,128},{8,136},{16,144},{24,152},{32,160},{40,168},{48,176},{56,1... | collective-permute-start | bytes 307208 | tf_op jit(solution)/shard_map/ppermute | solution.py:477
  7.5 0.5 collective-permute-start.2
  8.0 3.5 %collective-permute-start = (f32[7,48,128]{2,1,0:T(8,128)S(1)}, f32[7,48,128]{2,1,0:T(8,128)S(1)}, u32[]{:S(2)}, u32[]{:S(2)}) collective-permute-start(f32[7,48,128]{2,1,0:T(8,128)S(1)} %get-tuple-element.28), channel_id=1, source_target_pairs={{0,1},{1,2},{2,3},{3,4},{4,5},{5,6},{6,7},{8,9},{9,10},{10,11},{11... | collective-permute-start | bytes 516104 | tf_op jit(solution)/shard_map/ppermute | solution.py:484
  11.5 0.0 collective-permute-done.5.refs_4_
  11.5 4.5 %collective-permute-start.1 = (f32[7,48,128]{2,1,0:T(8,128)S(1)}, f32[7,48,128]{2,1,0:T(8,128)S(1)}, u32[]{:S(2)}, u32[]{:S(2)}) collective-permute-start(f32[7,48,128]{2,1,0:T(8,128)S(1)} %get-tuple-element.29), channel_id=1, source_target_pairs={{1,0},{2,1},{3,2},{4,3},{5,4},{6,5},{7,6},{9,8},{10,9},{11,10},{12... | collective-permute-start | bytes 516104 | tf_op jit(solution)/shard_map/ppermute | solution.py:484
  16.0 0.1 collective-permute-start.8
  16.1 0.0 collective-permute-done.3.refs_2_
  16.1 0.5 collective-permute-start.7
  16.6 0.0 collective-permute-done.2.refs_1_
  16.6 0.1 collective-permute-start.6
  16.8 0.1 copy.18.shares_ref
  17.0 0.1 copy.17.ids_ref
  17.1 0.3 collective-permute-done.8.refs_7_
  17.4 0.2 collective-permute-done.7.refs_6_
  17.6 0.4 collective-permute-done.6.refs_5_
  17.9 1.8 %relay.2 = (f32[200,128]{1,0:T(8,128)S(1)}, f32[200,128]{1,0:T(8,128)S(1)}, f32[200,128]{1,0:T(8,128)S(1)}, f32[200,128]{1,0:T(8,128)S(1)}) custom-call(s32[2]{0:T(128)S(1)} %pad_add_fusion.info.refs_0_, s32[32]{0:T(128)S(1)} %copy-done.7, s32[32,4,128]{2,1,0:T(4,128)S(1)} %copy.17.ids_ref, f32[32,4,128]{2,1,0:T(4,128)S(1)} %copy.18.shares_ref, ...), custom_call_target="tpu_custom_call" | custom-call | tf_op jit(solution)/shard_map/relay/pallas_call | solution.py:207
  19.8 3.4 %collective-permute-start.9 = (f32[200,128]{1,0:T(8,128)S(1)}, f32[200,128]{1,0:T(8,128)S(1)}, u32[]{:S(2)}, u32[]{:S(2)}) collective-permute-start(f32[200,128]{1,0:T(8,128)S(1)} %get-tuple-element.33), channel_id=1, source_target_pairs={{0,16},{8,24},{16,0},{24,8},{32,48},{40,56},{48,32},{56,40},{64,80... | collective-permute-start | bytes 307208 | tf_op jit(solution)/shard_map/ppermute | solution.py:477
  23.1 4.5 %collective-permute-start.10 = (f32[200,128]{1,0:T(8,128)S(1)}, f32[200,128]{1,0:T(8,128)S(1)}, u32[]{:S(2)}, u32[]{:S(2)}) collective-permute-start(f32[200,128]{1,0:T(8,128)S(1)} %get-tuple-element.34), channel_id=1, source_target_pairs={{0,32},{8,40},{16,48},{24,56},{32,0},{40,8},{48,16},{56,24},{64,96... | collective-permute-start | bytes 307208 | tf_op jit(solution)/shard_map/ppermute | solution.py:477
  27.6 0.0 collective-permute-start.11
  27.6 0.0 collective-permute-done.refs_9_
  27.7 0.0 copy-start.1
  27.7 9.8 %first_interior.1 = (f32[7,48,16,128]{3,2,1,0:T(8,128)S(1)}, f32[112,128]{1,0:T(8,128)S(1)}, f32[112,128]{1,0:T(8,128)S(1)}, f32[16,128]{1,0:T(8,128)S(1)}, f32[...) custom-call(s32[2]{0:T(128)S(1)} %pad_add_fusion.info.refs_0_, f32[7,7]{1,0:T(8,128)S(1)} %copy-done.6, ...), custom_call_target="tpu_custom_call" | custom-call | flops 30000000 | bytes 12000000 | tf_op jit(solution)/shard_map/first_interior/pallas_call | solution.py:368
  37.6 0.0 collective-permute-done.9.refs_1_
  37.6 0.0 collective-permute-done.10.refs_2_
  37.6 0.8 %boundary.1 = (f32[200,128]{1,0:T(8,128)S(1)}, f32[112,128]{1,0:T(8,128)S(1)}, f32[112,128]{1,0:T(8,128)S(1)}, f32[7,48,128]{2,1,0:T(8,128)S(1)}, f32[7,48,128]{2,1,0:T(8,128)S(1)}) custom-call(s32[2]{0:T(128)S(1)} %pad_add_fusion.info.refs_0_, f32[200,128]{1,0:T(8,128)S(1)} %get-tuple-element.31.refs_11_.refs_0_, ...), custom_call_target="tpu_custom_call" | custom-call | tf_op jit(solution)/shard_map/boundary/pallas_call | solution.py:433
  38.4 2.8 %collective-permute-start.16 = (f32[200,128]{1,0:T(8,128)S(1)}, f32[200,128]{1,0:T(8,128)S(1)}, u32[]{:S(2)}, u32[]{:S(2)}) collective-permute-start(f32[200,128]{1,0:T(8,128)S(1)} %get-tuple-element.44.refs_0_), channel_id=1, source_target_pairs={{0,192},{8,200},{16,208},{24,216},{32,224},{40,232},{48,240},{56,2... | collective-permute-start | bytes 307208 | tf_op jit(solution)/shard_map/ppermute | solution.py:477
  41.2 0.8 %collective-permute-start.15 = (f32[200,128]{1,0:T(8,128)S(1)}, f32[200,128]{1,0:T(8,128)S(1)}, u32[]{:S(2)}, u32[]{:S(2)}) collective-permute-start(f32[200,128]{1,0:T(8,128)S(1)} %get-tuple-element.44.refs_0_), channel_id=1, source_target_pairs={{0,128},{8,136},{16,144},{24,152},{32,160},{40,168},{48,176},{56,1... | collective-permute-start | bytes 307208 | tf_op jit(solution)/shard_map/ppermute | solution.py:477
  42.0 0.5 collective-permute-start.14
  42.6 2.8 %collective-permute-done.16.refs_3_ = f32[200,128]{1,0:T(8,128)S(1)} collective-permute-done((f32[200,128]{1,0:T(8,128)S(1)}, f32[200,128]{1,0:T(8,128)S(1)}, u32[]{:S(2)}, u32[]{:S(2)}) %collective-permute-start.16) | collective-permute-done | bytes 102432 | tf_op jit(solution)/shard_map/ppermute | solution.py:477
  45.4 0.0 collective-permute-start.20
  45.4 2.6 %collective-permute-done.15.refs_2_ = f32[200,128]{1,0:T(8,128)S(1)} collective-permute-done((f32[200,128]{1,0:T(8,128)S(1)}, f32[200,128]{1,0:T(8,128)S(1)}, u32[]{:S(2)}, u32[]{:S(2)}) %collective-permute-start.15) | collective-permute-done | bytes 102432 | tf_op jit(solution)/shard_map/ppermute | solution.py:477
  47.9 0.5 collective-permute-start.18
  48.4 1.9 %collective-permute-start.12 = (f32[7,48,128]{2,1,0:T(8,128)S(1)}, f32[7,48,128]{2,1,0:T(8,128)S(1)}, u32[]{:S(2)}, u32[]{:S(2)}) collective-permute-start(f32[7,48,128]{2,1,0:T(8,128)S(1)} %get-tuple-element.42), channel_id=1, source_target_pairs={{0,1},{1,2},{2,3},{3,4},{4,5},{5,6},{6,7},{8,9},{9,10},{10,11},{11... | collective-permute-start | bytes 516104 | tf_op jit(solution)/shard_map/ppermute | solution.py:484
  50.4 6.0 %collective-permute-start.13 = (f32[7,48,128]{2,1,0:T(8,128)S(1)}, f32[7,48,128]{2,1,0:T(8,128)S(1)}, u32[]{:S(2)}, u32[]{:S(2)}) collective-permute-start(f32[7,48,128]{2,1,0:T(8,128)S(1)} %get-tuple-element.43), channel_id=1, source_target_pairs={{1,0},{2,1},{3,2},{4,3},{5,4},{6,5},{7,6},{9,8},{10,9},{11,10},{12... | collective-permute-start | bytes 516104 | tf_op jit(solution)/shard_map/ppermute | solution.py:484
  56.4 0.0 collective-permute-done.19.refs_6_
  56.4 0.0 collective-permute-done.18.refs_5_
  56.4 1.8 %relay.3 = (f32[200,128]{1,0:T(8,128)S(1)}, f32[200,128]{1,0:T(8,128)S(1)}, f32[200,128]{1,0:T(8,128)S(1)}, f32[200,128]{1,0:T(8,128)S(1)}) custom-call(s32[2]{0:T(128)S(1)} %pad_add_fusion.info.refs_0_, s32[32]{0:T(128)S(1)} %copy-done.7, s32[32,4,128]{2,1,0:T(4,128)S(1)} %copy.17.ids_ref, f32[32,4,128]{2,1,0:T(4,128)S(1)} %copy.18.shares_ref, ...), custom_call_target="tpu_custom_call" | custom-call | tf_op jit(solution)/shard_map/relay/pallas_call | solution.py:207
  58.3 1.8 %collective-permute-start.21 = (f32[200,128]{1,0:T(8,128)S(1)}, f32[200,128]{1,0:T(8,128)S(1)}, u32[]{:S(2)}, u32[]{:S(2)}) collective-permute-start(f32[200,128]{1,0:T(8,128)S(1)} %get-tuple-element.48), channel_id=1, source_target_pairs={{0,16},{8,24},{16,0},{24,8},{32,48},{40,56},{48,32},{56,40},{64,80... | collective-permute-start | bytes 307208 | tf_op jit(solution)/shard_map/ppermute | solution.py:477
  60.1 4.5 %collective-permute-start.22 = (f32[200,128]{1,0:T(8,128)S(1)}, f32[200,128]{1,0:T(8,128)S(1)}, u32[]{:S(2)}, u32[]{:S(2)}) collective-permute-start(f32[200,128]{1,0:T(8,128)S(1)} %get-tuple-element.49), channel_id=1, source_target_pairs={{0,32},{8,40},{16,48},{24,56},{32,0},{40,8},{48,16},{56,24},{64,96... | collective-permute-start | bytes 307208 | tf_op jit(solution)/shard_map/ppermute | solution.py:477
  64.6 0.3 collective-permute-start.23
  64.9 0.0 collective-permute-done.12.refs_9_
  64.9 7.7 %second_interior.1 = f32[7,48,16,128]{3,2,1,0:T(8,128)S(1)} custom-call(s32[2]{0:T(128)S(1)} %pad_add_fusion.info.refs_0_, f32[7,7]{1,0:T(8,128)S(1)} %copy-done.6, f32[7,768,128]{2,1,0:T(8,128)S(1)} %bitcast.23, f32[7,48,16,128]{3,2,1,0:T(8,128)S(1)} %bitcast.21, f32[7,48,16,128]{3,2,1,0:T(8,128)} %bitcast.31, f32[48,16,128]{2,1,0:T(8,128)S(1)} %bitcast.25, ...), custom_call_target="tpu_custom_call" | custom-call | flops 30000000 | bytes 12000000 | tf_op jit(solution)/shard_map/second_interior/pallas_call | solution.py:368
  72.7 3.0 %correct_final.1 = f32[7,768,128]{2,1,0:T(8,128)} custom-call(s32[2]{0:T(128)S(1)} %pad_add_fusion.info.refs_0_, f32[7,768,128]{2,1,0:T(8,128)S(1)} %bitcast.22, f32[200,128]{1,0:T(8,128)S(1)} %get-tuple-element.45.refs_11_.refs_0_, f32[200,128]{1,0:T(8,128)S(1)} %collective-permute-done.21.refs_1_, f32[200,128]{1,0:T(8,128)S(1)} %collective-permute-done.22.refs_2_, ...), custom_call_target="tpu_custom_call" | custom-call | tf_op jit(solution)/shard_map/correct_final/pallas_call | solution.py:463
  (35 shorter events, 0.1 us)
Async XLA Ops:
  0.0 16.7 %copy-start.9 = (s32[32,8,4]{0,2,1:T(4,128)S(1)}, s32[32,8,4]{0,2,1:T(4,128)}, u32[]{:S(2)}) copy-start(s32[32,8,4]{0,2,1:T(4,128)} %param.21) | copy-start | bytes 12292
  0.0 16.8 %copy-start.8 = (s32[32,8,4]{0,2,1:T(4,128)S(1)}, s32[32,8,4]{0,2,1:T(4,128)}, u32[]{:S(2)}) copy-start(s32[32,8,4]{0,2,1:T(4,128)} %param.20) | copy-start | bytes 12292
  0.0 17.9 %copy-start.7 = (s32[32]{0:T(128)S(1)}, s32[32]{0:T(128)}, u32[]{:S(2)}) copy-start(s32[32]{0:T(128)} %partner.3) | copy-start | bytes 388
  0.0 27.6 %copy-start.6 = (f32[7,7]{1,0:T(8,128)S(1)}, f32[7,7]{1,0:T(8,128)}, u32[]{:S(2)}) copy-start(f32[7,7]{1,0:T(8,128)} %refs_1_.3) | copy-start | bytes 592
  0.1 1.8 %copy-start = (f32[7,1,48,16,128]{4,3,2,1,0:T(8,128)S(1)}, f32[7,1,48,16,128]{4,3,2,1,0:T(8,128)}, u32[]{:S(2)}) copy-start(f32[7,1,48,16,128]{4,3,2,1,0:T(8,128)} %param.11) | copy-start | bytes 8257540
  1.9 25.8 %copy-start.2 = (f32[1,48,16,128]{3,2,1,0:T(8,128)S(1)}, f32[1,48,16,128]{3,2,1,0:T(8,128)}, u32[]{:S(2)}) copy-start(f32[1,48,16,128]{3,2,1,0:T(8,128)} %param.14) | copy-start | bytes 1179652
  1.9 25.8 %copy-start.3 = (f32[1,48,16,128]{3,2,1,0:T(8,128)S(1)}, f32[1,48,16,128]{3,2,1,0:T(8,128)}, u32[]{:S(2)}) copy-start(f32[1,48,16,128]{3,2,1,0:T(8,128)} %param.15) | copy-start | bytes 1179652
  1.9 25.8 %copy-start.4 = (f32[1,48,16,128]{3,2,1,0:T(8,128)S(1)}, f32[1,48,16,128]{3,2,1,0:T(8,128)}, u32[]{:S(2)}) copy-start(f32[1,48,16,128]{3,2,1,0:T(8,128)} %param.16) | copy-start | bytes 1179652
  1.9 25.8 %copy-start.5 = (f32[7,16,128]{2,1,0:T(8,128)S(1)}, f32[7,16,128]{2,1,0:T(8,128)}, u32[]{:S(2)}) copy-start(f32[7,16,128]{2,1,0:T(8,128)} %refs_8_.3) | copy-start | bytes 172036
  3.8 7.7 %collective-permute-start.5 = (f32[200,128]{1,0:T(8,128)S(1)}, f32[200,128]{1,0:T(8,128)S(1)}, u32[]{:S(2)}, u32[]{:S(2)}) collective-permute-start(f32[200,128]{1,0:T(8,128)S(1)} %get-tuple-element.30.refs_0_), channel_id=1, source_target_pairs={{0,8},{8,0},{16,24},{24,16},{32,40},{40,32},{48,56},{56,48},{64,72... | collective-permute-start | bytes 307208 | tf_op jit(solution)/shard_map/ppermute | solution.py:477
  3.9 12.2 %collective-permute-start.4 = (f32[200,128]{1,0:T(8,128)S(1)}, f32[200,128]{1,0:T(8,128)S(1)}, u32[]{:S(2)}, u32[]{:S(2)}) collective-permute-start(f32[200,128]{1,0:T(8,128)S(1)} %get-tuple-element.30.refs_0_), channel_id=1, source_target_pairs={{0,192},{8,200},{16,208},{24,216},{32,224},{40,232},{48,240},{56,2... | collective-permute-start | bytes 307208 | tf_op jit(solution)/shard_map/ppermute | solution.py:477
  6.7 9.4 %collective-permute-start.3 = (f32[200,128]{1,0:T(8,128)S(1)}, f32[200,128]{1,0:T(8,128)S(1)}, u32[]{:S(2)}, u32[]{:S(2)}) collective-permute-start(f32[200,128]{1,0:T(8,128)S(1)} %get-tuple-element.30.refs_0_), channel_id=1, source_target_pairs={{0,128},{8,136},{16,144},{24,152},{32,160},{40,168},{48,176},{56,1... | collective-permute-start | bytes 307208 | tf_op jit(solution)/shard_map/ppermute | solution.py:477
  7.5 9.1 %collective-permute-start.2 = (f32[200,128]{1,0:T(8,128)S(1)}, f32[200,128]{1,0:T(8,128)S(1)}, u32[]{:S(2)}, u32[]{:S(2)}) collective-permute-start(f32[200,128]{1,0:T(8,128)S(1)} %get-tuple-element.30.refs_0_), channel_id=1, source_target_pairs={{0,64},{8,72},{16,80},{24,88},{32,96},{40,104},{48,112},{56,120},{... | collective-permute-start | bytes 307208 | tf_op jit(solution)/shard_map/ppermute | solution.py:477
  8.0 19.6 %collective-permute-start = (f32[7,48,128]{2,1,0:T(8,128)S(1)}, f32[7,48,128]{2,1,0:T(8,128)S(1)}, u32[]{:S(2)}, u32[]{:S(2)}) collective-permute-start(f32[7,48,128]{2,1,0:T(8,128)S(1)} %get-tuple-element.28), channel_id=1, source_target_pairs={{0,1},{1,2},{2,3},{3,4},{4,5},{5,6},{6,7},{8,9},{9,10},{10,11},{11... | collective-permute-start | bytes 516104 | tf_op jit(solution)/shard_map/ppermute | solution.py:484
  11.5 16.1 %collective-permute-start.1 = (f32[7,48,128]{2,1,0:T(8,128)S(1)}, f32[7,48,128]{2,1,0:T(8,128)S(1)}, u32[]{:S(2)}, u32[]{:S(2)}) collective-permute-start(f32[7,48,128]{2,1,0:T(8,128)S(1)} %get-tuple-element.29), channel_id=1, source_target_pairs={{1,0},{2,1},{3,2},{4,3},{5,4},{6,5},{7,6},{9,8},{10,9},{11,10},{12... | collective-permute-start | bytes 516104 | tf_op jit(solution)/shard_map/ppermute | solution.py:484
  16.0 1.4 %collective-permute-start.8 = (f32[200,128]{1,0:T(8,128)S(1)}, f32[200,128]{1,0:T(8,128)S(1)}, u32[]{:S(2)}, u32[]{:S(2)}) collective-permute-start(f32[200,128]{1,0:T(8,128)S(1)} %collective-permute-done.4.refs_3_), channel_id=1, source_target_pairs={{0,8},{8,0},{16,24},{24,16},{32,40},{40,32},{48,56},{56,48},{64,72... | collective-permute-start | bytes 307208 | tf_op jit(solution)/shard_map/ppermute | solution.py:477
  16.1 1.4 %collective-permute-start.7 = (f32[200,128]{1,0:T(8,128)S(1)}, f32[200,128]{1,0:T(8,128)S(1)}, u32[]{:S(2)}, u32[]{:S(2)}) collective-permute-start(f32[200,128]{1,0:T(8,128)S(1)} %collective-permute-done.3.refs_2_), channel_id=1, source_target_pairs={{0,8},{8,0},{16,24},{24,16},{32,40},{40,32},{48,56},{56,48},{64,72... | collective-permute-start | bytes 307208 | tf_op jit(solution)/shard_map/ppermute | solution.py:477
  16.6 1.3 %collective-permute-start.6 = (f32[200,128]{1,0:T(8,128)S(1)}, f32[200,128]{1,0:T(8,128)S(1)}, u32[]{:S(2)}, u32[]{:S(2)}) collective-permute-start(f32[200,128]{1,0:T(8,128)S(1)} %collective-permute-done.2.refs_1_), channel_id=1, source_target_pairs={{0,8},{8,0},{16,24},{24,16},{32,40},{40,32},{48,56},{56,48},{64,72... | collective-permute-start | bytes 307208 | tf_op jit(solution)/shard_map/ppermute | solution.py:477
  19.8 17.8 %collective-permute-start.9 = (f32[200,128]{1,0:T(8,128)S(1)}, f32[200,128]{1,0:T(8,128)S(1)}, u32[]{:S(2)}, u32[]{:S(2)}) collective-permute-start(f32[200,128]{1,0:T(8,128)S(1)} %get-tuple-element.33), channel_id=1, source_target_pairs={{0,16},{8,24},{16,0},{24,8},{32,48},{40,56},{48,32},{56,40},{64,80... | collective-permute-start | bytes 307208 | tf_op jit(solution)/shard_map/ppermute | solution.py:477
  23.1 14.4 %collective-permute-start.10 = (f32[200,128]{1,0:T(8,128)S(1)}, f32[200,128]{1,0:T(8,128)S(1)}, u32[]{:S(2)}, u32[]{:S(2)}) collective-permute-start(f32[200,128]{1,0:T(8,128)S(1)} %get-tuple-element.34), channel_id=1, source_target_pairs={{0,32},{8,40},{16,48},{24,56},{32,0},{40,8},{48,16},{56,24},{64,96... | collective-permute-start | bytes 307208 | tf_op jit(solution)/shard_map/ppermute | solution.py:477
  27.6 10.0 %collective-permute-start.11 = (f32[200,128]{1,0:T(8,128)S(1)}, f32[200,128]{1,0:T(8,128)S(1)}, u32[]{:S(2)}, u32[]{:S(2)}) collective-permute-start(f32[200,128]{1,0:T(8,128)S(1)} %get-tuple-element.35), channel_id=1, source_target_pairs={{0,48},{8,56},{16,32},{24,40},{32,16},{40,24},{48,0},{56,8},{64,11... | collective-permute-start | bytes 307208 | tf_op jit(solution)/shard_map/ppermute | solution.py:477
  27.7 37.2 %copy-start.1 = (f32[7,1,48,16,128]{4,3,2,1,0:T(8,128)S(1)}, f32[7,1,48,16,128]{4,3,2,1,0:T(8,128)}, u32[]{:S(2)}) copy-start(f32[7,1,48,16,128]{4,3,2,1,0:T(8,128)} %param.12) | copy-start | bytes 8257540
  38.4 7.0 %collective-permute-start.16 = (f32[200,128]{1,0:T(8,128)S(1)}, f32[200,128]{1,0:T(8,128)S(1)}, u32[]{:S(2)}, u32[]{:S(2)}) collective-permute-start(f32[200,128]{1,0:T(8,128)S(1)} %get-tuple-element.44.refs_0_), channel_id=1, source_target_pairs={{0,192},{8,200},{16,208},{24,216},{32,224},{40,232},{48,240},{56,2... | collective-permute-start | bytes 307208 | tf_op jit(solution)/shard_map/ppermute | solution.py:477
  41.2 6.7 %collective-permute-start.15 = (f32[200,128]{1,0:T(8,128)S(1)}, f32[200,128]{1,0:T(8,128)S(1)}, u32[]{:S(2)}, u32[]{:S(2)}) collective-permute-start(f32[200,128]{1,0:T(8,128)S(1)} %get-tuple-element.44.refs_0_), channel_id=1, source_target_pairs={{0,128},{8,136},{16,144},{24,152},{32,160},{40,168},{48,176},{56,1... | collective-permute-start | bytes 307208 | tf_op jit(solution)/shard_map/ppermute | solution.py:477
  42.0 5.9 %collective-permute-start.14 = (f32[200,128]{1,0:T(8,128)S(1)}, f32[200,128]{1,0:T(8,128)S(1)}, u32[]{:S(2)}, u32[]{:S(2)}) collective-permute-start(f32[200,128]{1,0:T(8,128)S(1)} %get-tuple-element.44.refs_0_), channel_id=1, source_target_pairs={{0,64},{8,72},{16,80},{24,88},{32,96},{40,104},{48,112},{56,120},{... | collective-permute-start | bytes 307208 | tf_op jit(solution)/shard_map/ppermute | solution.py:477
  42.6 7.8 %collective-permute-start.17 = (f32[200,128]{1,0:T(8,128)S(1)}, f32[200,128]{1,0:T(8,128)S(1)}, u32[]{:S(2)}, u32[]{:S(2)}) collective-permute-start(f32[200,128]{1,0:T(8,128)S(1)} %get-tuple-element.44.refs_0_), channel_id=1, source_target_pairs={{0,8},{8,0},{16,24},{24,16},{32,40},{40,32},{48,56},{56,48},{64,72... | collective-permute-start | bytes 307208 | tf_op jit(solution)/shard_map/ppermute | solution.py:477
  45.4 11.1 %collective-permute-start.20 = (f32[200,128]{1,0:T(8,128)S(1)}, f32[200,128]{1,0:T(8,128)S(1)}, u32[]{:S(2)}, u32[]{:S(2)}) collective-permute-start(f32[200,128]{1,0:T(8,128)S(1)} %collective-permute-done.16.refs_3_), channel_id=1, source_target_pairs={{0,8},{8,0},{16,24},{24,16},{32,40},{40,32},{48,56},{56,48},{64,72... | collective-permute-start | bytes 307208 | tf_op jit(solution)/shard_map/ppermute | solution.py:477
  47.9 8.5 %collective-permute-start.19 = (f32[200,128]{1,0:T(8,128)S(1)}, f32[200,128]{1,0:T(8,128)S(1)}, u32[]{:S(2)}, u32[]{:S(2)}) collective-permute-start(f32[200,128]{1,0:T(8,128)S(1)} %collective-permute-done.15.refs_2_), channel_id=1, source_target_pairs={{0,8},{8,0},{16,24},{24,16},{32,40},{40,32},{48,56},{56,48},{64,72... | collective-permute-start | bytes 307208 | tf_op jit(solution)/shard_map/ppermute | solution.py:477
  47.9 8.5 %collective-permute-start.18 = (f32[200,128]{1,0:T(8,128)S(1)}, f32[200,128]{1,0:T(8,128)S(1)}, u32[]{:S(2)}, u32[]{:S(2)}) collective-permute-start(f32[200,128]{1,0:T(8,128)S(1)} %collective-permute-done.14.refs_1_), channel_id=1, source_target_pairs={{0,8},{8,0},{16,24},{24,16},{32,40},{40,32},{48,56},{56,48},{64,72... | collective-permute-start | bytes 307208 | tf_op jit(solution)/shard_map/ppermute | solution.py:477
  48.4 16.4 %collective-permute-start.12 = (f32[7,48,128]{2,1,0:T(8,128)S(1)}, f32[7,48,128]{2,1,0:T(8,128)S(1)}, u32[]{:S(2)}, u32[]{:S(2)}) collective-permute-start(f32[7,48,128]{2,1,0:T(8,128)S(1)} %get-tuple-element.42), channel_id=1, source_target_pairs={{0,1},{1,2},{2,3},{3,4},{4,5},{5,6},{6,7},{8,9},{9,10},{10,11},{11... | collective-permute-start | bytes 516104 | tf_op jit(solution)/shard_map/ppermute | solution.py:484
  50.4 14.5 %collective-permute-start.13 = (f32[7,48,128]{2,1,0:T(8,128)S(1)}, f32[7,48,128]{2,1,0:T(8,128)S(1)}, u32[]{:S(2)}, u32[]{:S(2)}) collective-permute-start(f32[7,48,128]{2,1,0:T(8,128)S(1)} %get-tuple-element.43), channel_id=1, source_target_pairs={{1,0},{2,1},{3,2},{4,3},{5,4},{6,5},{7,6},{9,8},{10,9},{11,10},{12... | collective-permute-start | bytes 516104 | tf_op jit(solution)/shard_map/ppermute | solution.py:484
  58.3 14.3 %collective-permute-start.21 = (f32[200,128]{1,0:T(8,128)S(1)}, f32[200,128]{1,0:T(8,128)S(1)}, u32[]{:S(2)}, u32[]{:S(2)}) collective-permute-start(f32[200,128]{1,0:T(8,128)S(1)} %get-tuple-element.48), channel_id=1, source_target_pairs={{0,16},{8,24},{16,0},{24,8},{32,48},{40,56},{48,32},{56,40},{64,80... | collective-permute-start | bytes 307208 | tf_op jit(solution)/shard_map/ppermute | solution.py:477
  60.1 12.5 %collective-permute-start.22 = (f32[200,128]{1,0:T(8,128)S(1)}, f32[200,128]{1,0:T(8,128)S(1)}, u32[]{:S(2)}, u32[]{:S(2)}) collective-permute-start(f32[200,128]{1,0:T(8,128)S(1)} %get-tuple-element.49), channel_id=1, source_target_pairs={{0,32},{8,40},{16,48},{24,56},{32,0},{40,8},{48,16},{56,24},{64,96... | collective-permute-start | bytes 307208 | tf_op jit(solution)/shard_map/ppermute | solution.py:477
  64.6 8.1 %collective-permute-start.23 = (f32[200,128]{1,0:T(8,128)S(1)}, f32[200,128]{1,0:T(8,128)S(1)}, u32[]{:S(2)}, u32[]{:S(2)}) collective-permute-start(f32[200,128]{1,0:T(8,128)S(1)} %get-tuple-element.50), channel_id=1, source_target_pairs={{0,48},{8,56},{16,32},{24,40},{32,16},{40,24},{48,0},{56,8},{64,11... | collective-permute-start | bytes 307208 | tf_op jit(solution)/shard_map/ppermute | solution.py:477
